TPU v7x, 512 devices: a whole 4x4x16 slice. The times are simulated.
512 devices in a mesh: graph: 32 (over z, core), feat: 16 (over y, x).
Axes of the slice: x: 4, y: 4, z: 16, core: 2. Of those that a mesh axis runs over, the one named last changes fastest.
Arguments:
- source_feats: bfloat16 [1024, 32768], P('feat', 'graph'), may hold values from -6 to 6
- vertex_feats: bfloat16 [1024, 1024], P('feat', 'graph'), may hold values from -6 to 6
- block_values: bfloat16 [2048, 128, 128], P('graph'), as said below
- block_target: int32 [2048], P('graph'), may hold values from 0 to 7, as said below
- block_source: int32 [2048], P('graph'), may hold values from 0 to 7
- block_count: int32 [32], P('graph'), may hold values from 1 to 64, as said below
- seed_rows: int32 [1024], P(('graph', 'feat')), may hold values from 0 to 31, as said below
- seed_weights: bfloat16 [1024, 32], P(('graph', 'feat')), may hold values from -1 to 1
- neigh_one: bfloat16 [1024, 256], P('feat'), may hold values from -0.1875 to 0.1875
- self_one: bfloat16 [1024, 256], P('feat'), may hold values from -0.1875 to 0.1875
- bias_one: float32 [256], replicated, may hold values from -3 to 3
- self_two: bfloat16 [256, 256], replicated, may hold values from -0.375 to 0.375
- neigh_two: bfloat16 [256, 256], replicated, may hold values from -0.375 to 0.375
- bias_two: float32 [256], replicated, may hold values from -3 to 3
- output_grad: bfloat16 [1024, 256], P(('graph', 'feat')), may hold values from -0.1875 to 0.1875
Outputs:
- out_two: bfloat16 [1024, 256], P(('graph', 'feat'))
- grad_neigh_one: float32 [1024, 256], P('feat')
- grad_self_one: float32 [1024, 256], P('feat')
- grad_bias_one: float32 [256], replicated
- grad_self_two: float32 [256, 256], replicated
- grad_neigh_two: float32 [256, 256], replicated
- grad_bias_two: float32 [256], replicated
Inputs may be any that keep to these rules, and one draw needn't show every extreme that they name: Within a partition the 64 slots name distinct (block_target, block_source) pairs. `block_count`: some partition uses all 64 slots. `seed_rows`: distinct within a partition. `block_values`: zero where a pair has no edge.
All inputs are finite; a program needn't handle non-finite values.
Results may differ from a plain program's by a relative error of at most 0.022.
Values sent between devices are 32-bit elements; how exact they have to be, the bound alone decides.
A program may use at most 64 MiB of HBM per device.

v0:
```python
import jax
import jax.numpy as jnp
from jax import lax
from jax.sharding import PartitionSpec as P

norm_eps = 1e-05


def normalize(pre_act):
    rect = jnp.maximum(pre_act, 0.0)
    msq = jnp.mean(rect * rect, axis=-1, keepdims=True)
    inverse = lax.rsqrt(msq + norm_eps)
    return (rect, inverse, (rect * inverse).astype(jnp.bfloat16))


def norm_backward(d_hidden, pre_act, rect, inverse):
    factor = jnp.mean(d_hidden * rect, axis=-1, keepdims=True) * inverse * inverse
    return jnp.where(pre_act > 0, (d_hidden - rect * factor) * inverse, jnp.zeros_like(pre_act))


def body(
    source_feats,
    vertex_feats,
    block_values,
    block_target,
    block_source,
    block_count,
    seed_rows,
    seed_weights,
    neigh_one,
    self_one,
    bias_one,
    self_two,
    neigh_two,
    bias_two,
    output_grad,
):
    highest = lax.Precision.HIGHEST
    contract_first = (((0,), (0,)), ((), ()))
    width_part = source_feats.shape[0]
    owned_rows = vertex_feats.shape[1]
    hop_rows = owned_rows * lax.axis_size("graph")
    target_blocks = hop_rows // 128
    source_view = source_feats.reshape(width_part, source_feats.shape[1] // 128, 128)
    group_size = min(16, block_values.shape[0])
    live_count = block_count[0]
    rounds = (live_count + group_size - 1) // group_size
    target_ids = jnp.arange(target_blocks, dtype=jnp.int32)

    def one_round(turn, total):
        first = turn * group_size
        values = lax.dynamic_slice_in_dim(block_values, first, group_size, 0)
        targets = lax.dynamic_slice_in_dim(block_target, first, group_size, 0)
        sources = lax.dynamic_slice_in_dim(block_source, first, group_size, 0)
        live = first + jnp.arange(group_size, dtype=jnp.int32) < live_count
        picked = jnp.take(source_view, sources, axis=1)
        terms = jnp.einsum("fkj,kij->kfi", picked, values, preferred_element_type=jnp.float32)
        routing = ((targets[None, :] == target_ids[:, None]) & live[None, :]).astype(jnp.float32)
        return total + jnp.einsum("dk,kfi->fdi", routing, terms, precision=highest)

    agg_blocks = lax.fori_loop(
        0, rounds, one_round, jnp.zeros((width_part, target_blocks, 128), jnp.float32)
    )
    agg_feats = agg_blocks.reshape(width_part, hop_rows)
    neigh_wide = neigh_one.astype(jnp.float32)
    columns = agg_feats
    owned = lax.psum_scatter(
        lax.dot_general(columns, neigh_wide, contract_first, precision=highest),
        "graph",
        scatter_dimension=0,
        tiled=True,
    )
    owned = owned + lax.dot_general(
        vertex_feats, self_one, contract_first, preferred_element_type=jnp.float32
    )
    pre_act = lax.psum(owned, "feat") + bias_one
    rect, inverse, hidden_one = normalize(pre_act)
    self_vals = jnp.take(hidden_one, seed_rows, axis=0)
    agg_two = jnp.dot(seed_weights, hidden_one, preferred_element_type=jnp.float32).astype(
        jnp.bfloat16
    )
    out_full = jnp.dot(self_vals, self_two, preferred_element_type=jnp.float32) + jnp.dot(
        agg_two, neigh_two, preferred_element_type=jnp.float32
    )
    out_two = (out_full + bias_two).astype(jnp.bfloat16)
    local_self = lax.dot_general(
        self_vals, output_grad, contract_first, preferred_element_type=jnp.float32
    )
    local_neigh = lax.dot_general(
        agg_two, output_grad, contract_first, preferred_element_type=jnp.float32
    )
    local_bias = jnp.sum(output_grad.astype(jnp.float32), axis=0)
    grad_self_two, grad_neigh_two, grad_bias_two = lax.psum(
        (local_self, local_neigh, local_bias), ("graph", "feat")
    )
    contract_last = (((1,), (1,)), ((), ()))
    d_self = lax.dot_general(
        output_grad, self_two, contract_last, preferred_element_type=jnp.float32
    )
    d_agg = lax.dot_general(
        output_grad, neigh_two, contract_last, preferred_element_type=jnp.float32
    )
    row_ids = jnp.arange(owned_rows, dtype=jnp.int32)
    picker = (seed_rows[:, None] == row_ids[None, :]).astype(jnp.float32)
    d_hidden = lax.dot_general(picker, d_self, contract_first, precision=highest)
    d_hidden = d_hidden + lax.dot_general(
        seed_weights.astype(jnp.float32), d_agg, contract_first, precision=highest
    )
    d_hidden = lax.psum(d_hidden, "feat")
    d_pre = norm_backward(d_hidden, pre_act, rect, inverse)
    local_vertex = jnp.dot(vertex_feats.astype(jnp.float32), d_pre, precision=highest)
    local_bias_one = jnp.sum(d_pre, axis=0)
    columns = agg_feats
    partial_neigh = jnp.dot(
        columns, lax.all_gather(d_pre, "graph", axis=0, tiled=True), precision=highest
    )
    grad_neigh_one, grad_self_one, grad_bias_one = lax.psum(
        (partial_neigh, local_vertex, local_bias_one), "graph"
    )
    return (
        out_two,
        grad_neigh_one,
        grad_self_one,
        grad_bias_one,
        grad_self_two,
        grad_neigh_two,
        grad_bias_two,
    )


def solution(mesh):
    in_specs = (
        P("feat", "graph"),
        P("feat", "graph"),
        P("graph", None, None),
        P("graph"),
        P("graph"),
        P("graph"),
        P(("graph", "feat")),
        P(("graph", "feat"), None),
        P("feat", None),
        P("feat", None),
        P(),
        P(),
        P(),
        P(),
        P(("graph", "feat"), None),
    )
    out_specs = (P(("graph", "feat"), None), P("feat", None), P("feat", None), P(), P(), P(), P())
    return jax.shard_map(body, mesh=mesh, in_specs=in_specs, out_specs=out_specs, check_vma=False)
```

profile of v0, /device:TPU:1, one launch (start us, length us, event | category | flops | bytes accessed | tf_op | source)
XLA Modules:
  0.0 1027.1 jit_solution(14840383479560792179)
XLA Ops:
  8.2 19.8 %while.11 = (s32[]{:T(128)}, f32[64,8,128]{2,1,0:T(8,128)S(1)}, s32[]{:T(128)}, s32[64]{0:T(128)}, bf16[64,8,128]{2,0,1:T(8,128)(2,1)S(1)}, /*index=5*/bf16[64,1...) while((s32[]{:T(128)}, f32[64,8,128]{2,1,0:T(8,128)S(1)}, ...), condition=%wide.region_1.2_spmd.clone, body=%wide.region_0.1_spmd.clone.sunk | while | flops 46335364 | bytes 2888383 | solution.py:61
  8.2 1.4 compare_and_fusion.3
  10.2 1.5 fusion.68
  11.7 0.7 dynamic_slice.19
  13.1 1.4 compare_and_fusion.3
  15.1 1.5 fusion.68
  16.7 0.7 dynamic_slice.19
  18.1 1.4 compare_and_fusion.3
  20.1 1.5 fusion.68
  21.6 0.7 dynamic_slice.19
  23.0 1.4 compare_and_fusion.3
  25.0 1.5 fusion.68
  26.6 0.7 dynamic_slice.19
  28.1 1.6 fusion.22
  30.4 0.9 fusion.17
  31.2 108.7 %reduce-scatter.2.cloned.1.call-done = f32[32,256]{1,0:T(8,128)} async-done(((f32[1024,256]{1,0:T(8,128)}), f32[32,256]{1,0:T(8,128)}) %reduce-scatter.2.cloned.1.call-update) | async-done | bytes 32784 | tf_op jit(solution)/shard_map/reduce_scatter | solution.py:67
  140.0 1.5 convolution_add_fusion
  141.5 113.8 %all-reduce.11.cloned.1.call-done = (f32[32,256]{1,0:T(8,128)}, f32[32,256]{1,0:T(8,128)}) async-done(((f32[32,256]{1,0:T(8,128)}, f32[32,256]{1,0:T(8,128)}), (f32[32,256]{1,0:T(8,128)}, f32[32,256]{1,0:T(8,128)})) %all-reduce.11.cloned.1.call-update) | async-done | bytes 65552 | tf_op jit(solution)/shard_map/psum | solution.py:76
  255.3 0.9 multiply_reduce_fusion
  256.2 1.5 fusion.32
  257.8 105.3 %psum.63 = f32[256]{0:T(256)} all-reduce(f32[256]{0:T(256)S(1)} %convert_reduce_fusion), channel_id=1, replica_groups=mesh['graph'=32,'feat'=16] {'graph','feat'}, use_global_device_ids=true, to_apply=%region_14.15 | all-reduce | flops 256 | bytes 2048 | tf_op jit(solution)/shard_map/psum | solution.py:93
  364.0 0.9 fusion.35
  364.9 1.0 fusion.30
  366.0 1.6 convolution_bitcast_fusion.1
  367.6 2.5 fusion.20
  370.9 47.1 %psum.60 = f32[256]{0:T(256)} all-reduce(f32[256]{0:T(256)S(1)} %get-tuple-element.109), channel_id=1, replica_groups=mesh['graph'=32,'feat'=16] {'graph'}, use_global_device_ids=true, to_apply=%region_10.11 | all-reduce | flops 256 | bytes 2048 | tf_op jit(solution)/shard_map/psum | solution.py:117
  417.9 400.2 %all-reduce.7.cloned.1.call-done = (f32[256,256]{1,0:T(8,128)}, f32[256,256]{1,0:T(8,128)}) async-done(((f32[256,256]{1,0:T(8,128)}, f32[256,256]{1,0:T(8,128)}), (f32[256,256]{1,0:T(8,128)}, f32[256,256]{1,0:T(8,128)})) %all-reduce.7.cloned.1.call-update) | async-done | bytes 524304 | tf_op jit(solution)/shard_map/psum | solution.py:93
  818.1 196.1 %all-reduce.9.cloned.1.call-done = (f32[64,256]{1,0:T(8,128)}, f32[64,256]{1,0:T(8,128)}) async-done(((f32[64,256]{1,0:T(8,128)}, f32[64,256]{1,0:T(8,128)}), (f32[64,256]{1,0:T(8,128)}, f32[64,256]{1,0:T(8,128)})) %all-reduce.9.cloned.1.call-update) | async-done | bytes 131088 | tf_op jit(solution)/shard_map/psum | solution.py:117
  1014.2 1.5 copy.52
  1015.7 1.5 copy.53
  1017.2 1.7 copy.54
  1018.9 1.7 copy.55
  (59 shorter events, 7.8 us)
Async XLA Ops:
  7.2 0.9 copy-start
  7.2 132.8 %reduce-scatter.2.cloned.1.call-start = ((), (), s32[]{:S(2)}) async-start(), calls=%async_computation.1 | async-start | bytes 1081344 | tf_op jit(solution)/shard_map/reduce_scatter | solution.py:67
  8.1 19.9 %copy-start.5 = (bf16[64,256]{1,0:T(8,128)(2,1)S(1)}, bf16[64,256]{1,0:T(8,128)(2,1)}, u32[]{:S(2)}) copy-start(bf16[64,256]{1,0:T(8,128)(2,1)} %param.25) | copy-start | bytes 98308
  27.9 1.8 copy-start.2
  28.0 1.8 copy-start.6
  28.0 1.9 copy-start.10
  28.0 2.2 copy-start.1
  28.0 2.4 copy-start.8
  28.0 112.0 %copy-start.3 = (bf16[64,256]{1,0:T(8,128)(2,1)S(1)}, bf16[64,256]{1,0:T(8,128)(2,1)}, u32[]{:S(2)}) copy-start(bf16[64,256]{1,0:T(8,128)(2,1)} %param.26) | copy-start | bytes 98308
  28.0 111.9 %copy-start.4 = (bf16[64,32]{0,1:T(8,128)(2,1)S(1)}, bf16[64,32]{0,1:T(8,128)(2,1)}, u32[]{:S(2)}) copy-start(bf16[64,32]{0,1:T(8,128)(2,1)} %param.18) | copy-start | bytes 12292
  28.0 227.3 %copy-start.7 = (f32[256]{0:T(256)S(1)}, f32[256]{0:T(256)}, u32[]{:S(2)}) copy-start(f32[256]{0:T(256)} %param.27) | copy-start | bytes 3076
  29.7 340.5 %copy-start.9 = (f32[256]{0:T(256)S(1)}, f32[256]{0:T(256)}, u32[]{:S(2)}) copy-start(f32[256]{0:T(256)} %param.30) | copy-start | bytes 3076
  29.7 225.7 %all-reduce.11.cloned.1.call-start = ((), (), s32[]{:S(2)}) async-start(), calls=%async_computation.5 | async-start | bytes 131072 | tf_op jit(solution)/shard_map/psum | solution.py:76
  141.5 226.1 %all-gather.2.cloned.1.call-start = ((), (), s32[]{:S(2)}) async-start(), calls=%async_computation.2 | async-start | bytes 1081344 | tf_op jit(solution)/shard_map/all_gather | solution.py:115
  257.7 560.4 %all-reduce.7.cloned.1.call-start = ((), (), s32[]{:S(2)}) async-start(), calls=%async_computation.3 | async-start | bytes 1048576 | tf_op jit(solution)/shard_map/psum | solution.py:93
  365.9 648.3 %all-reduce.9.cloned.1.call-start = ((), (), s32[]{:S(2)}) async-start(), calls=%async_computation.4 | async-start | bytes 262144 | tf_op jit(solution)/shard_map/psum | solution.py:117
Sparse Core Ops, SparseCore 0:
  29.8 110.1 reduce-scatter.1
  144.1 111.2 all-reduce.10
  258.0 71.8 all-gather.1
  366.0 452.0 all-reduce.6
  821.1 193.0 all-reduce.8
where the time goes:
time: 1030 us
  waiting for transfers between devices  819 us (80%)
  blocking collectives  152 us (15%)
  matrix products  20.4 us (2%)
  between operations  14.7 us (1%)
  local copies, waits for them, and re-layouts  12.4 us (1%)
    psum x1, waiting for transfers between devices, body(): lax.psum((local_self, local_neigh, local_bias), ('graph', 'feat'))  400 us
    psum x1, waiting for transfers between devices, body(): lax.psum((partial_neigh, local_vertex, local_bias_one), 'graph')  196 us
    psum x1, waiting for transfers between devices, body(): pre_act = lax.psum(owned, 'feat') + bias_one  114 us
    reduce_scatter x1, waiting for transfers between devices, body(): lax.psum_scatter(lax.dot_general(columns, neigh_wide, contract_first, pre...  109 us
    psum x1, blocking collectives, body(): lax.psum((local_self, local_neigh, local_bias), ('graph', 'feat'))  105 us
    psum x1, blocking collectives, body(): lax.psum((partial_neigh, local_vertex, local_bias_one), 'graph')  47.1 us
  transfers between devices with their start and end apart: 5, of which 4 were waited for; matrix products, arithmetic and copies ran while one was open for 1% of the time, Pallas kernels for 0%

commit v1 on v0

v1 whole, which is shorter than its diff:
```python
import jax
import jax.numpy as jnp
from jax import lax
from jax.experimental import pallas as pl
from jax.experimental.pallas import tpu as pltpu
from jax.sharding import PartitionSpec as P

MESH = pl.DeviceIdType.MESH
HIGHEST = lax.Precision.HIGHEST
norm_eps = 1e-05
f32, bf16 = jnp.float32, jnp.bfloat16

NZ, NX, NF = 16, 4, 16
FAR_FIRST = (8, 7, 9, 6, 10, 5, 11, 4, 12, 3, 13, 2, 14, 1, 15)
BLOCK_ORDER = (4, 5, 3, 6, 2, 7, 1, 0)
TILES, EXTRA = 21, 5
PAIR0, EARLY, ZSUM0, XY0, XY1, PAIR1, ZSUM1, ZSUMX, ZALL, ZALLX, FALL, PAIR2, PAIR3 = (0, 4, 5, 6, 7, 8, 9, 10, 11, 12, 13, 14, 15)
PHASES = 16


def dot(a, b, ca, cb, precision=None):
    return lax.dot_general(
        a, b, (((ca,), (cb,)), ((), ())), preferred_element_type=f32, precision=precision
    )


def main_kernel(
    target_ref,
    source_ref,
    count_ref,
    rows_ref,
    src_ref,
    val_hbm,
    vert_ref,
    sw_ref,
    neigh1_ref,
    self1_ref,
    bias1_ref,
    self2_ref,
    neigh2_ref,
    bias2_ref,
    og_ref,
    out_ref,
    fin_ref,
    gfin_ref,
    val,
    order_v,
    order_s,
    early,
    agg,
    sib,
    zin,
    xy,
    hid_scr,
    g_scr,
    share,
    sib2,
    red,
    zred,
    zredx,
    local_sem,
    ssem,
    rsem,
):
    g = lax.axis_index("graph")
    f = lax.axis_index("feat")
    z, c = g // 2, g % 2
    y, x = f // 4, f % 4
    sibling = (g + 1 - 2 * c, f)

    def z_peer(off):
        return (2 * lax.rem(z + off, NZ) + c, f)

    def f_peer(off):
        return (g, lax.rem(f + off, NF))

    def x_peer(off):
        return (g, 4 * y + lax.rem(x + off, NX))

    def y_peer(off):
        return (g, 4 * lax.rem(y + off, NX) + x)

    def send(src, dst, phase, dev):
        pltpu.make_async_remote_copy(
            src_ref=src,
            dst_ref=dst,
            send_sem=ssem.at[phase],
            recv_sem=rsem.at[phase],
            device_id=dev,
            device_id_type=MESH,
        ).start()

    def recv(ref, phase):
        pltpu.make_async_remote_copy(
            src_ref=ref,
            dst_ref=ref,
            send_sem=ssem.at[phase],
            recv_sem=rsem.at[phase],
            device_id=sibling,
            device_id_type=MESH,
        ).wait_recv()

    def sent(ref, phase):
        pltpu.make_async_remote_copy(
            src_ref=ref,
            dst_ref=ref,
            send_sem=ssem.at[phase],
            recv_sem=rsem.at[phase],
            device_id=sibling,
            device_id_type=MESH,
        ).wait_send()

    fetch = pltpu.make_async_copy(val_hbm, val, local_sem.at[0])
    fetch.start()

    barrier = pltpu.get_barrier_semaphore()
    pl.semaphore_signal(barrier, inc=1, device_id=sibling, device_id_type=MESH)
    for off in FAR_FIRST:
        pl.semaphore_signal(barrier, inc=1, device_id=z_peer(off), device_id_type=MESH)
    for off in range(1, NF):
        pl.semaphore_signal(barrier, inc=1, device_id=f_peer(off), device_id_type=MESH)

    pair = target_ref[...] * 8 + source_ref[...]
    slot = lax.broadcasted_iota(jnp.int32, (64, 64), 1)
    code = jnp.where(slot >= count_ref[0], slot + 64, slot)
    hit = pair == lax.broadcasted_iota(jnp.int32, (64, 64), 0)
    picked = jnp.where(hit, code, 0)
    order_v[...] = jnp.sum(picked.T, axis=0, keepdims=True)
    to_scalar = pltpu.make_async_copy(order_v, order_s, local_sem.at[1])
    to_scalar.start()

    hop = lax.broadcasted_iota(jnp.int32, (1, 32), 1)
    og_own = og_ref[...].astype(f32)
    sw_own = sw_ref[...].astype(f32)
    hot_own = jnp.concatenate(
        [(hop == rows_ref[0]).astype(f32), (hop == rows_ref[1]).astype(f32)], axis=0
    )
    blank = jnp.zeros((2, 64), f32)
    early_own = jnp.concatenate(
        [
            og_own[:, 0:128],
            og_own[:, 128:256],
            jnp.concatenate([sw_own, hot_own, blank], axis=1),
            jnp.zeros((2, 128), f32),
        ],
        axis=0,
    )
    early[f] = early_own

    doubled = jnp.concatenate([src_ref[...], src_ref[...]], axis=0)
    low_lanes = lax.broadcasted_iota(jnp.int32, (16, 128), 1) < 64
    to_scalar.wait()
    fetch.wait()

    def block(delta):
        d = lax.rem(z // 2 + delta, 8)
        cols = []
        for s in range(8):
            k = order_s[0, d * 8 + s]
            live = jnp.where(k < 64, 1.0, 0.0).astype(bf16)
            cols.append(val[lax.rem(k, 64)] * live)
        wide = dot(jnp.concatenate(cols, axis=1), doubled, 1, 1)
        for q in range(4):
            top, bottom = wide[32 * q : 32 * q + 16], wide[32 * q + 16 : 32 * q + 32]
            agg[q % 2, 2 * d + q // 2] = jnp.where(low_lanes, top, bottom)

    def pair_rows(group):
        return [2 * lax.rem(z // 2 + delta, 8) for delta in BLOCK_ORDER[2 * group : 2 * group + 2]]

    def pair_send(group):
        for row in pair_rows(group):
            send(agg.at[1 - c, pl.ds(row, 2)], sib.at[pl.ds(row, 2)], PAIR0 + group, sibling)

    def pair_done(group):
        recv(sib.at[pl.ds(0, 4)], PAIR0 + group)
        for delta in BLOCK_ORDER[2 * group : 2 * group + 2]:
            row = 2 * lax.rem(z // 2 + delta, 8)
            if delta:
                for h in range(2):
                    agg[c, row + h] = agg[c, row + h] + sib[row + h]
                    send(agg.at[c, row + h], zin.at[z], ZSUM0, (2 * (row + h) + c, f))
            else:
                other = row + 1 - z % 2
                agg[c, other] = agg[c, other] + sib[other]
                send(agg.at[c, other], zin.at[z], ZSUM0, (2 * other + c, f))
                zin[z] = agg[c, z] + sib[z]

    for group in range(4):
        block(BLOCK_ORDER[2 * group])
        block(BLOCK_ORDER[2 * group + 1])
        if group == 0:
            pl.semaphore_wait(barrier, 31)
        pair_send(group)
        if group == 0:
            for off in range(1, NF):
                send(early.at[f], early.at[f], EARLY, f_peer(off))
        if group:
            pair_done(group - 1)
    pair_done(3)

    recv(early.at[pl.ds(0, NF - 1)], EARLY)
    og_all = jnp.concatenate(
        [
            jnp.concatenate([early[:, 0, :], early[:, 1, :]], axis=0),
            jnp.concatenate([early[:, 2, :], early[:, 3, :]], axis=0),
        ],
        axis=1,
    )
    sw_hot = jnp.concatenate([early[:, 4, :], early[:, 5, :]], axis=0)
    sw_all, hot_all = sw_hot[:, 0:32], sw_hot[:, 32:64]
    og_16 = og_all.astype(bf16)
    d_self = dot(og_16, self2_ref[...], 1, 1)
    d_agg = dot(og_16, neigh2_ref[...], 1, 1)
    d_hidden = dot(hot_all, d_self, 0, 0, HIGHEST) + dot(sw_all, d_agg, 0, 0, HIGHEST)
    bias2_part = jnp.sum(og_all, axis=0, keepdims=True)

    own_term = dot(vert_ref[...], self1_ref[...], 0, 0)

    recv(zin.at[pl.ds(0, NZ - 1)], ZSUM0)
    packed = zin[0]
    for i in range(1, NZ):
        packed = packed + zin[i]
    agg_own = jnp.concatenate([packed[:, 0:64], packed[:, 64:128]], axis=0)
    agg_hi = agg_own.astype(bf16)
    agg_lo = (agg_own - agg_hi.astype(f32)).astype(bf16)
    halves = jnp.concatenate([agg_hi, agg_lo], axis=0)
    product = dot(halves, neigh1_ref[...], 1, 0)
    partial = product[0:32] + product[32:64] + own_term

    xy[0, 0, x] = partial[:, 0:128]
    xy[0, 1, y] = partial[:, 128:256]
    for off in (2, 1, 3):
        send(xy.at[0, 0, x], xy.at[0, 0, x], XY0, x_peer(off))
        send(xy.at[0, 1, y], xy.at[0, 1, y], XY0, y_peer(off))
    recv(xy.at[0, :, pl.ds(0, 3)], XY0)
    xy[1, 0, y] = (xy[0, 0, 0] + xy[0, 0, 1]) + (xy[0, 0, 2] + xy[0, 0, 3])
    xy[1, 1, x] = (xy[0, 1, 0] + xy[0, 1, 1]) + (xy[0, 1, 2] + xy[0, 1, 3])
    for off in (2, 1, 3):
        send(xy.at[1, 0, y], xy.at[1, 0, y], XY1, y_peer(off))
        send(xy.at[1, 1, x], xy.at[1, 1, x], XY1, x_peer(off))
    recv(xy.at[1, :, pl.ds(0, 3)], XY1)
    left = (xy[1, 0, 0] + xy[1, 0, 1]) + (xy[1, 0, 2] + xy[1, 0, 3])
    right = (xy[1, 1, 0] + xy[1, 1, 1]) + (xy[1, 1, 2] + xy[1, 1, 3])
    pre_act = jnp.concatenate([left, right], axis=1) + bias1_ref[...]

    rect = jnp.maximum(pre_act, 0.0)
    msq = jnp.mean(rect * rect, axis=-1, keepdims=True)
    inverse = lax.rsqrt(msq + norm_eps)
    hidden = (rect * inverse).astype(bf16)
    factor = jnp.mean(d_hidden * rect, axis=-1, keepdims=True) * inverse * inverse
    d_pre = jnp.where(pre_act > 0, (d_hidden - rect * factor) * inverse, 0.0)
    d_pre_16 = d_pre.astype(bf16)

    hid_scr[0] = hidden[:, 0:128]
    hid_scr[1] = hidden[:, 128:256]
    mixer = jnp.where(f < 8, hot_all, sw_all).astype(bf16)
    mixed = dot(mixer, hid_scr[lax.rem(f, 8) // 4], 1, 0).astype(bf16)
    g_scr[...] = dot(mixed, og_16, 0, 0)
    g_rows = g_scr[pl.ds(pl.multiple_of(32 * lax.rem(f, 4), 32), 32), :]

    grad_neigh = dot(agg_hi, d_pre_16, 0, 0)
    grad_self = dot(vert_ref[...], d_pre_16, 1, 0)
    bias1_part = jnp.sum(d_pre, axis=0, keepdims=True)

    for a in range(8):
        for b in range(2):
            rows, cols = slice(8 * a, 8 * a + 8), slice(128 * b, 128 * b + 128)
            share[0, 2 * a + b] = grad_neigh[rows, cols]
            share[1, 2 * a + b] = grad_self[rows, cols]
    for a in range(4):
        for b in range(2):
            rows, cols = slice(8 * a, 8 * a + 8), slice(128 * b, 128 * b + 128)
            share[a // 2, 16 + 2 * (a % 2) + b] = g_rows[rows, cols]
    bias_tile = jnp.concatenate(
        [
            bias1_part[:, 0:128],
            bias1_part[:, 128:256],
            bias2_part[:, 0:128],
            bias2_part[:, 128:256],
            jnp.zeros((4, 128), f32),
        ],
        axis=0,
    )
    share[0, 20] = bias_tile
    share[1, 20] = jnp.zeros((8, 128), f32)

    send(share.at[1 - c], sib2, PAIR1, sibling)
    recv(sib2, PAIR1)
    red[...] = share[c] + sib2[...]
    for off in FAR_FIRST:
        to = lax.rem(z + off, NZ)
        send(red.at[to], zred.at[z], ZSUM1, (2 * to + c, f))
    zred[z] = red[z]
    for e in range(EXTRA):
        owner = 3 * e

        @pl.when(z != owner)
        def _():
            send(red.at[16 + e], zredx.at[z], ZSUMX, (2 * owner + c, f))

    pad = jnp.zeros((6, 32), f32)
    sw_8 = jnp.concatenate([sw_own, pad], axis=0).astype(bf16)
    hot_8 = jnp.concatenate([hot_own, pad], axis=0).astype(bf16)
    self_vals = dot(hot_8, hidden, 1, 0).astype(bf16)
    agg_two = dot(sw_8, hidden, 1, 0).astype(bf16)
    out_full = dot(self_vals, self2_ref[...], 1, 0) + dot(agg_two, neigh2_ref[...], 1, 0)
    out_ref[...] = (out_full + bias2_ref[...]).astype(bf16)[0:2]

    recv(zred.at[pl.ds(0, NZ - 1)], ZSUM1)
    total = zred[0]
    for i in range(1, NZ):
        total = total + zred[i]
    fin_ref[c, z] = total
    for off in FAR_FIRST:
        send(fin_ref.at[c, z], fin_ref.at[c, z], ZALL, z_peer(off))

    owns_extra = jnp.logical_and(lax.rem(z, 3) == 0, z < 3 * EXTRA)
    mine = 16 + z // 3

    @pl.when(owns_extra)
    def _():
        recv(zredx.at[pl.ds(0, NZ - 1)], ZSUMX)
        zredx[z] = red[mine]
        more = zredx[0]
        for i in range(1, NZ):
            more = more + zredx[i]
        fin_ref[c, mine] = more
        for off in FAR_FIRST:
            send(fin_ref.at[c, mine], fin_ref.at[c, mine], ZALLX, z_peer(off))
        recv(fin_ref.at[c, pl.ds(0, EXTRA - 1)], ZALLX)

    @pl.when(jnp.logical_not(owns_extra))
    def _():
        recv(fin_ref.at[c, pl.ds(0, EXTRA)], ZALLX)

    for off in (10, 2, 8, 6, 14, 9, 11, 5, 7, 13, 15, 1, 3, 4, 12):
        send(fin_ref.at[c, pl.ds(16, 4)], gfin_ref.at[c, f], FALL, f_peer(off))
    for t in range(4):
        gfin_ref[c, f, t] = fin_ref[c, 16 + t]
    recv(fin_ref.at[c, pl.ds(0, NZ - 1)], ZALL)
    send(fin_ref.at[c], fin_ref.at[c], PAIR2, sibling)
    recv(gfin_ref.at[c, pl.ds(0, NF - 1)], FALL)
    send(gfin_ref.at[c], gfin_ref.at[c], PAIR3, sibling)
    recv(fin_ref.at[1 - c], PAIR2)
    recv(gfin_ref.at[1 - c], PAIR3)

    for group in range(4):
        sent(sib.at[pl.ds(0, 4)], PAIR0 + group)
    sent(early.at[pl.ds(0, NF - 1)], EARLY)
    sent(zin.at[pl.ds(0, NZ - 1)], ZSUM0)
    for phase in (XY0, XY1):
        sent(xy.at[0, :, pl.ds(0, 3)], phase)
    sent(sib2, PAIR1)
    sent(zred.at[pl.ds(0, NZ - 1)], ZSUM1)

    @pl.when(owns_extra)
    def _():
        sent(zredx.at[pl.ds(0, EXTRA - 1)], ZSUMX)
        sent(zredx.at[pl.ds(0, NZ - 1)], ZALLX)

    @pl.when(jnp.logical_not(owns_extra))
    def _():
        sent(zredx.at[pl.ds(0, EXTRA)], ZSUMX)

    sent(zred.at[pl.ds(0, NZ - 1)], ZALL)
    sent(gfin_ref.at[c, pl.ds(0, NF - 1)], FALL)
    sent(fin_ref.at[c], PAIR2)
    sent(gfin_ref.at[c], PAIR3)


def lay_out_kernel(
    fin_ref, gfin_ref, out_in_ref, out_ref, neigh1_ref, self1_ref, bias1_ref, self2_ref, neigh2_ref, bias2_ref
):
    out_ref[...] = out_in_ref[...]
    for a in range(8):
        for b in range(2):
            rows, cols = slice(8 * a, 8 * a + 8), slice(128 * b, 128 * b + 128)
            neigh1_ref[rows, cols] = fin_ref[0, 2 * a + b]
            self1_ref[rows, cols] = fin_ref[1, 2 * a + b]
    bias = fin_ref[0, 20]
    bias1_ref[...] = jnp.concatenate([bias[0:1], bias[1:2]], axis=1)
    bias2_ref[...] = jnp.concatenate([bias[2:3], bias[3:4]], axis=1)
    for i in range(NF):
        ref = self2_ref if i < 8 else neigh2_ref
        for core in range(2):
            for t in range(4):
                row = 32 * (i % 8) + 16 * core + 8 * (t // 2)
                col = 128 * (t % 2)
                ref[row : row + 8, col : col + 128] = gfin_ref[core, i, t]


def body(
    source_feats,
    vertex_feats,
    block_values,
    block_target,
    block_source,
    block_count,
    seed_rows,
    seed_weights,
    neigh_one,
    self_one,
    bias_one,
    self_two,
    neigh_two,
    bias_two,
    output_grad,
):
    vmem = pl.BlockSpec(memory_space=pltpu.VMEM)
    smem = pl.BlockSpec(memory_space=pltpu.SMEM)
    hbm = pl.BlockSpec(memory_space=pl.ANY)
    out_two, fin, gfin = pl.pallas_call(
        main_kernel,
        out_shape=(
            jax.ShapeDtypeStruct((2, 256), bf16),
            jax.ShapeDtypeStruct((2, TILES, 8, 128), f32),
            jax.ShapeDtypeStruct((2, NF, 4, 8, 128), f32),
        ),
        in_specs=[vmem, vmem, smem, smem, vmem, hbm] + [vmem] * 9,
        out_specs=(vmem, vmem, vmem),
        scratch_shapes=[
            pltpu.VMEM((64, 128, 128), bf16),
            pltpu.VMEM((1, 64), jnp.int32),
            pltpu.SMEM((1, 64), jnp.int32),
            pltpu.VMEM((NF, 8, 128), f32),
            pltpu.VMEM((2, NZ, 16, 128), f32),
            pltpu.VMEM((NZ, 16, 128), f32),
            pltpu.VMEM((NZ, 16, 128), f32),
            pltpu.VMEM((2, 2, NX, 32, 128), f32),
            pltpu.VMEM((2, 32, 128), bf16),
            pltpu.VMEM((128, 256), f32),
            pltpu.VMEM((2, TILES, 8, 128), f32),
            pltpu.VMEM((TILES, 8, 128), f32),
            pltpu.VMEM((TILES, 8, 128), f32),
            pltpu.VMEM((NZ, 8, 128), f32),
            pltpu.VMEM((NZ, 8, 128), f32),
            pltpu.SemaphoreType.DMA((2,)),
            pltpu.SemaphoreType.DMA((PHASES,)),
            pltpu.SemaphoreType.DMA((PHASES,)),
        ],
        compiler_params=pltpu.CompilerParams(
            collective_id=1, has_side_effects=True, vmem_limit_bytes=32 * 2**20
        ),
    )(
        block_target.reshape(1, 64),
        block_source.reshape(1, 64),
        block_count,
        seed_rows,
        source_feats,
        block_values,
        vertex_feats,
        seed_weights,
        neigh_one,
        self_one,
        bias_one.reshape(1, 256),
        self_two,
        neigh_two,
        bias_two.reshape(1, 256),
        output_grad,
    )
    outs = pl.pallas_call(
        lay_out_kernel,
        out_shape=(
            jax.ShapeDtypeStruct((2, 256), bf16),
            jax.ShapeDtypeStruct((64, 256), f32),
            jax.ShapeDtypeStruct((64, 256), f32),
            jax.ShapeDtypeStruct((1, 256), f32),
            jax.ShapeDtypeStruct((256, 256), f32),
            jax.ShapeDtypeStruct((256, 256), f32),
            jax.ShapeDtypeStruct((1, 256), f32),
        ),
        in_specs=[vmem] * 3,
        out_specs=(vmem,) * 7,
    )(fin, gfin, out_two)
    out_two, neigh1, self1, bias1, self2, neigh2, bias2 = outs
    return out_two, neigh1, self1, bias1.reshape(256), self2, neigh2, bias2.reshape(256)


def solution(mesh):
    in_specs = (
        P("feat", "graph"),
        P("feat", "graph"),
        P("graph", None, None),
        P("graph"),
        P("graph"),
        P("graph"),
        P(("graph", "feat")),
        P(("graph", "feat"), None),
        P("feat", None),
        P("feat", None),
        P(),
        P(),
        P(),
        P(),
        P(("graph", "feat"), None),
    )
    out_specs = (P(("graph", "feat"), None), P("feat", None), P("feat", None), P(), P(), P(), P())
    return jax.shard_map(body, mesh=mesh, in_specs=in_specs, out_specs=out_specs, check_vma=False)
```

time: 1030 us -> 76.6 us (0.07)
  waiting for transfers between devices: 819 us -> 0 us
  blocking collectives: 152 us -> 0 us
  Pallas kernels: 0 us -> 61.5 us
  matrix products: 20.4 us -> 0 us
  between operations: 14.7 us -> 1.32 us
    psum x3 -> x0, waiting for transfers between devices: 710 us -> none  [the longest x1 400 us: body(): lax.psum((local_self, local_neigh, local_bias), ('graph', 'feat'))]
    psum x2 -> x0, blocking collectives: 152 us -> none  [the longest x1 105 us: body(): lax.psum((local_self, local_neigh, local_bias), ('graph', 'feat'))]
    reduce_scatter x1 -> x0, waiting for transfers between devices: 109 us -> none  [body(): lax.psum_scatter(lax.dot_general(columns, neigh_wide, contract_first, pre...]
    pallas_call x0 -> x2, Pallas kernels: none -> 61.5 us  [the longest x1 59.6 us: body(): pl.pallas_call(main_kernel, out_shape=(jax.ShapeDtypeStruct((2, 256), bf1...]
    dot_general x21 -> x0, matrix products: 20.4 us -> none  [the longest x4 6.15 us: one_round(): jnp.einsum('fkj,kij->kfi', picked, values, preferred_element_type=jnp.flo...]
  transfers between devices with their start and end apart: 5 -> 0, of which waited for: 4 -> 0; matrix products, arithmetic and copies ran while one was open for 1% -> 0% of each run, Pallas kernels for 0% -> 0%
where the time goes in v1:
time: 76.6 us; the launch traced here: 76.1 us
  Pallas kernels  61.5 us (80%)
  local copies, waits for them, and re-layouts  13.3 us (17%)
  between operations  1.32 us (2%)
    pallas_call x1, Pallas kernels, body(): pl.pallas_call(main_kernel, out_shape=(jax.ShapeDtypeStruct((2, 256), bf1...  59.6 us
    unnamed x33, local copies, waits for them, and re-layouts  13.3 us
    pallas_call x1, Pallas kernels, body(): pl.pallas_call(lay_out_kernel, out_shape=(jax.ShapeDtypeStruct((2, 256),...  1.93 us

profile of v1, /device:TPU:1, one launch (start us, length us, event | category | flops | bytes accessed | tf_op | source)
XLA Modules:
  0.0 76.1 jit_solution(13356129101380550250)
XLA Ops:
  1.3 0.8 %copy.22.vert_ref = bf16[64,32]{1,0:T(8,128)(2,1)S(1)} copy(bf16[64,32]{0,1:T(8,128)(2,1)} %param.16) | data formatting | bytes 8192 | tf_op args[1]
  2.1 0.0 copy-start
  2.1 1.6 %copy-done = bf16[64,128,128]{2,1,0:T(8,128)(2,1)S(1)} copy-done((bf16[64,128,128]{2,1,0:T(8,128)(2,1)S(1)}, bf16[64,128,128]{2,1,0:T(8,128)(2,1)}, u32[]{:S(2)}) %copy-start) | copy-done | bytes 2097176
  3.7 0.9 %copy-done.3 = bf16[64,1024]{1,0:T(8,128)(2,1)S(1)} copy-done((bf16[64,1024]{1,0:T(8,128)(2,1)S(1)}, bf16[64,1024]{1,0:T(8,128)(2,1)}, u32[]{:S(2)}) %copy-start.3) | copy-done | bytes 131096
  4.6 0.0 copy-start.4
  4.6 0.9 %copy-done.4 = bf16[256,256]{1,0:T(8,128)(2,1)S(1)} copy-done((bf16[256,256]{1,0:T(8,128)(2,1)S(1)}, bf16[256,256]{1,0:T(8,128)(2,1)}, u32[]{:S(2)}) %copy-start.4) | copy-done | bytes 131096
  5.5 0.0 copy-start.5
  5.5 0.9 %copy-done.5 = bf16[256,256]{1,0:T(8,128)(2,1)S(1)} copy-done((bf16[256,256]{1,0:T(8,128)(2,1)S(1)}, bf16[256,256]{1,0:T(8,128)(2,1)}, u32[]{:S(2)}) %copy-start.5) | copy-done | bytes 131096
  6.4 0.0 copy-start.6
  6.4 0.8 copy-done.6
  7.1 0.0 copy-start.7
  7.1 0.8 copy-done.7
  7.9 0.0 copy-start.8
  7.9 0.7 copy-done.8
  8.6 0.0 copy-start.9
  8.6 0.7 copy-done.9
  9.3 0.7 copy-done.10
  9.9 0.0 copy-start.12
  9.9 0.7 copy-done.12
  10.6 0.0 copy-start.13
  10.6 0.7 copy-done.13
  11.2 0.0 copy-start.14
  11.2 0.7 copy-done.14
  11.9 0.0 copy-start.15
  11.9 0.7 copy-done.15
  12.6 59.6 %shard_map.198 = (bf16[2,256]{1,0:T(2,128)(2,1)S(1)}, f32[2,21,8,128]{3,2,1,0:T(8,128)S(1)}, f32[2,16,4,8,128]{4,3,2,1,0:T(8,128)S(1)}) custom-call(s32[1,64]{1,0:T(1,128)S(1)} %bitcast.8, s32[1,64]{1,0:T(1,128)S(1)} %bitcast.9, s32[1]{0:T(128)S(6)} %copy.23.count_ref, s32[2]{0:T(128)S(1)} %copy-done.14, bf16[64,1024]{1,0:T(8,128)(2,1)S(1)} %copy-done.3, ...), custom_call_target="tpu_custom_call" | custom-call | tf_op jit(solution)/shard_map/pallas_call | solution.py:412
  72.2 0.0 copy-start.1
  72.2 0.8 %copy-done.1 = f32[2,16,4,8,128]{4,3,2,1,0:T(8,128)} copy-done((f32[2,16,4,8,128]{4,3,2,1,0:T(8,128)}, f32[2,16,4,8,128]{4,3,2,1,0:T(8,128)S(1)}, u32[]{:S(2)}) %copy-start.1) | copy-done | bytes 524312
  72.9 0.0 copy-start.2
  72.9 0.7 copy-done.2
  73.6 0.6 copy-done.11
  74.2 1.9 %shard_map.199 = (bf16[2,256]{1,0:T(2,128)(2,1)}, f32[64,256]{1,0:T(8,128)}, f32[64,256]{1,0:T(8,128)}, f32[1,256]{1,0:T(1,128)}, f32[256,256]{1,0:T(8,128)}, /*index=5*/f32[256,256]{1,0:T(8,128)}, f32[1,256]{1,0:T(1,128)}) custom-call(f32[2,21,8,128]{3,2,1,0:T(8,128)} %copy-done.2, f32[2,16,4,8,128]{4,3,2,1,0:T(8,128)} %copy-done.1, bf16[2,256]{1,0:T(2,128)(2,1)} %copy-done.11), custom_call_target="tpu_custom_call" | custom-call | tf_op jit(solution)/shard_map/pallas_call | solution.py:461
  (3 shorter events, 0.0 us)
Async XLA Ops:
  2.1 1.6 %copy-start = (bf16[64,128,128]{2,1,0:T(8,128)(2,1)S(1)}, bf16[64,128,128]{2,1,0:T(8,128)(2,1)}, u32[]{:S(2)}) copy-start(bf16[64,128,128]{2,1,0:T(8,128)(2,1)} %val_hbm.1) | copy-start | bytes 6291460
  3.7 0.9 %copy-start.3 = (bf16[64,1024]{1,0:T(8,128)(2,1)S(1)}, bf16[64,1024]{1,0:T(8,128)(2,1)}, u32[]{:S(2)}) copy-start(bf16[64,1024]{1,0:T(8,128)(2,1)} %src_ref.1) | copy-start | bytes 393220
  4.6 0.9 %copy-start.4 = (bf16[256,256]{1,0:T(8,128)(2,1)S(1)}, bf16[256,256]{1,0:T(8,128)(2,1)}, u32[]{:S(2)}) copy-start(bf16[256,256]{1,0:T(8,128)(2,1)} %self2_ref.1) | copy-start | bytes 393220
  5.5 0.9 %copy-start.5 = (bf16[256,256]{1,0:T(8,128)(2,1)S(1)}, bf16[256,256]{1,0:T(8,128)(2,1)}, u32[]{:S(2)}) copy-start(bf16[256,256]{1,0:T(8,128)(2,1)} %neigh2_ref.1) | copy-start | bytes 393220
  6.4 0.8 copy-start.6
  7.1 0.8 copy-start.7
  7.9 0.7 copy-start.8
  8.6 0.7 copy-start.9
  9.3 0.7 copy-start.10
  9.9 0.7 copy-start.12
  10.6 0.7 copy-start.13
  11.2 0.7 copy-start.14
  11.9 0.7 copy-start.15
  72.2 0.8 %copy-start.1 = (f32[2,16,4,8,128]{4,3,2,1,0:T(8,128)}, f32[2,16,4,8,128]{4,3,2,1,0:T(8,128)S(1)}, u32[]{:S(2)}) copy-start(f32[2,16,4,8,128]{4,3,2,1,0:T(8,128)S(1)} %get-tuple-element.18.gfin_ref) | copy-start | bytes 1572868
  72.9 0.7 copy-start.2
  73.6 0.6 copy-start.11

commit v2 on v1

--- a/solution.py
+++ b/solution.py
@@ -25,25 +25,37 @@
 
 
 def main_kernel(
+    target_hbm,
+    source_hbm,
+    count_hbm,
+    rows_hbm,
+    src_hbm,
+    val_hbm,
+    vert_hbm,
+    neigh1_hbm,
+    self1_hbm,
+    bias1_hbm,
+    self2_hbm,
+    neigh2_hbm,
+    bias2_hbm,
+    sw_ref,
+    og_ref,
+    out_ref,
+    fin_ref,
+    gfin_ref,
     target_ref,
     source_ref,
     count_ref,
     rows_ref,
     src_ref,
-    val_hbm,
+    val,
     vert_ref,
-    sw_ref,
     neigh1_ref,
     self1_ref,
     bias1_ref,
     self2_ref,
     neigh2_ref,
     bias2_ref,
-    og_ref,
-    out_ref,
-    fin_ref,
-    gfin_ref,
-    val,
     order_v,
     order_s,
     early,
@@ -110,8 +122,30 @@
             device_id_type=MESH,
         ).wait_send()
 
-    fetch = pltpu.make_async_copy(val_hbm, val, local_sem.at[0])
-    fetch.start()
+    pending = []
+
+    def drain():
+        for ref, phase in pending:
+            sent(ref, phase)
+
+    fetches = []
+    for src, dst in (
+        (target_hbm, target_ref),
+        (source_hbm, source_ref),
+        (count_hbm, count_ref),
+        (val_hbm, val),
+        (src_hbm, src_ref),
+        (rows_hbm, rows_ref),
+        (vert_hbm, vert_ref),
+        (self1_hbm, self1_ref),
+        (neigh1_hbm, neigh1_ref),
+        (self2_hbm, self2_ref),
+        (neigh2_hbm, neigh2_ref),
+        (bias1_hbm, bias1_ref),
+        (bias2_hbm, bias2_ref),
+    ):
+        fetches.append(pltpu.make_async_copy(src, dst, local_sem.at[1 + len(fetches)]))
+        fetches[-1].start()
 
     barrier = pltpu.get_barrier_semaphore()
     pl.semaphore_signal(barrier, inc=1, device_id=sibling, device_id_type=MESH)
@@ -120,15 +154,18 @@
     for off in range(1, NF):
         pl.semaphore_signal(barrier, inc=1, device_id=f_peer(off), device_id_type=MESH)
 
+    for i in range(3):
+        fetches[i].wait()
     pair = target_ref[...] * 8 + source_ref[...]
     slot = lax.broadcasted_iota(jnp.int32, (64, 64), 1)
     code = jnp.where(slot >= count_ref[0], slot + 64, slot)
     hit = pair == lax.broadcasted_iota(jnp.int32, (64, 64), 0)
     picked = jnp.where(hit, code, 0)
     order_v[...] = jnp.sum(picked.T, axis=0, keepdims=True)
-    to_scalar = pltpu.make_async_copy(order_v, order_s, local_sem.at[1])
+    to_scalar = pltpu.make_async_copy(order_v, order_s, local_sem.at[0])
     to_scalar.start()
 
+    fetches[5].wait()
     hop = lax.broadcasted_iota(jnp.int32, (1, 32), 1)
     og_own = og_ref[...].astype(f32)
     sw_own = sw_ref[...].astype(f32)
@@ -147,10 +184,11 @@
     )
     early[f] = early_own
 
+    fetches[4].wait()
     doubled = jnp.concatenate([src_ref[...], src_ref[...]], axis=0)
     low_lanes = lax.broadcasted_iota(jnp.int32, (16, 128), 1) < 64
     to_scalar.wait()
-    fetch.wait()
+    fetches[3].wait()
 
     def block(delta):
         d = lax.rem(z // 2 + delta, 8)
@@ -197,7 +235,11 @@
         if group:
             pair_done(group - 1)
     pair_done(3)
-
+    pending += [(sib.at[pl.ds(0, 4)], PAIR0 + group) for group in range(4)]
+    pending += [(early.at[pl.ds(0, NF - 1)], EARLY), (zin.at[pl.ds(0, NZ - 1)], ZSUM0)]
+
+    for i in range(6, 13):
+        fetches[i].wait()
     recv(early.at[pl.ds(0, NF - 1)], EARLY)
     og_all = jnp.concatenate(
         [
@@ -214,7 +256,7 @@
     d_hidden = dot(hot_all, d_self, 0, 0, HIGHEST) + dot(sw_all, d_agg, 0, 0, HIGHEST)
     bias2_part = jnp.sum(og_all, axis=0, keepdims=True)
 
-    own_term = dot(vert_ref[...], self1_ref[...], 0, 0)
+    own_term = dot(vert_ref[...], self1_ref[...], 1, 0)
 
     recv(zin.at[pl.ds(0, NZ - 1)], ZSUM0)
     packed = zin[0]
@@ -232,12 +274,14 @@
     for off in (2, 1, 3):
         send(xy.at[0, 0, x], xy.at[0, 0, x], XY0, x_peer(off))
         send(xy.at[0, 1, y], xy.at[0, 1, y], XY0, y_peer(off))
+    pending.append((xy.at[0, :, pl.ds(0, 3)], XY0))
     recv(xy.at[0, :, pl.ds(0, 3)], XY0)
     xy[1, 0, y] = (xy[0, 0, 0] + xy[0, 0, 1]) + (xy[0, 0, 2] + xy[0, 0, 3])
     xy[1, 1, x] = (xy[0, 1, 0] + xy[0, 1, 1]) + (xy[0, 1, 2] + xy[0, 1, 3])
     for off in (2, 1, 3):
         send(xy.at[1, 0, y], xy.at[1, 0, y], XY1, y_peer(off))
         send(xy.at[1, 1, x], xy.at[1, 1, x], XY1, x_peer(off))
+    pending.append((xy.at[1, :, pl.ds(0, 3)], XY1))
     recv(xy.at[1, :, pl.ds(0, 3)], XY1)
     left = (xy[1, 0, 0] + xy[1, 0, 1]) + (xy[1, 0, 2] + xy[1, 0, 3])
     right = (xy[1, 1, 0] + xy[1, 1, 1]) + (xy[1, 1, 2] + xy[1, 1, 3])
@@ -259,7 +303,7 @@
     g_rows = g_scr[pl.ds(pl.multiple_of(32 * lax.rem(f, 4), 32), 32), :]
 
     grad_neigh = dot(agg_hi, d_pre_16, 0, 0)
-    grad_self = dot(vert_ref[...], d_pre_16, 1, 0)
+    grad_self = dot(vert_ref[...], d_pre_16, 0, 0)
     bias1_part = jnp.sum(d_pre, axis=0, keepdims=True)
 
     for a in range(8):
@@ -285,12 +329,14 @@
     share[1, 20] = jnp.zeros((8, 128), f32)
 
     send(share.at[1 - c], sib2, PAIR1, sibling)
+    pending.append((sib2, PAIR1))
     recv(sib2, PAIR1)
     red[...] = share[c] + sib2[...]
     for off in FAR_FIRST:
         to = lax.rem(z + off, NZ)
         send(red.at[to], zred.at[z], ZSUM1, (2 * to + c, f))
     zred[z] = red[z]
+    pending.append((zred.at[pl.ds(0, NZ - 1)], ZSUM1))
     for e in range(EXTRA):
         owner = 3 * e
 
@@ -328,10 +374,13 @@
         for off in FAR_FIRST:
             send(fin_ref.at[c, mine], fin_ref.at[c, mine], ZALLX, z_peer(off))
         recv(fin_ref.at[c, pl.ds(0, EXTRA - 1)], ZALLX)
+        sent(zredx.at[pl.ds(0, EXTRA - 1)], ZSUMX)
+        sent(zredx.at[pl.ds(0, NZ - 1)], ZALLX)
 
     @pl.when(jnp.logical_not(owns_extra))
     def _():
         recv(fin_ref.at[c, pl.ds(0, EXTRA)], ZALLX)
+        sent(zredx.at[pl.ds(0, EXTRA)], ZSUMX)
 
     for off in (10, 2, 8, 6, 14, 9, 11, 5, 7, 13, 15, 1, 3, 4, 12):
         send(fin_ref.at[c, pl.ds(16, 4)], gfin_ref.at[c, f], FALL, f_peer(off))
@@ -344,28 +393,13 @@
     recv(fin_ref.at[1 - c], PAIR2)
     recv(gfin_ref.at[1 - c], PAIR3)
 
-    for group in range(4):
-        sent(sib.at[pl.ds(0, 4)], PAIR0 + group)
-    sent(early.at[pl.ds(0, NF - 1)], EARLY)
-    sent(zin.at[pl.ds(0, NZ - 1)], ZSUM0)
-    for phase in (XY0, XY1):
-        sent(xy.at[0, :, pl.ds(0, 3)], phase)
-    sent(sib2, PAIR1)
-    sent(zred.at[pl.ds(0, NZ - 1)], ZSUM1)
-
-    @pl.when(owns_extra)
-    def _():
-        sent(zredx.at[pl.ds(0, EXTRA - 1)], ZSUMX)
-        sent(zredx.at[pl.ds(0, NZ - 1)], ZALLX)
-
-    @pl.when(jnp.logical_not(owns_extra))
-    def _():
-        sent(zredx.at[pl.ds(0, EXTRA)], ZSUMX)
-
-    sent(zred.at[pl.ds(0, NZ - 1)], ZALL)
-    sent(gfin_ref.at[c, pl.ds(0, NF - 1)], FALL)
-    sent(fin_ref.at[c], PAIR2)
-    sent(gfin_ref.at[c], PAIR3)
+    pending += [
+        (zred.at[pl.ds(0, NZ - 1)], ZALL),
+        (gfin_ref.at[c, pl.ds(0, NF - 1)], FALL),
+        (fin_ref.at[c], PAIR2),
+        (gfin_ref.at[c], PAIR3),
+    ]
+    drain()
 
 
 def lay_out_kernel(
@@ -407,7 +441,6 @@
     output_grad,
 ):
     vmem = pl.BlockSpec(memory_space=pltpu.VMEM)
-    smem = pl.BlockSpec(memory_space=pltpu.SMEM)
     hbm = pl.BlockSpec(memory_space=pl.ANY)
     out_two, fin, gfin = pl.pallas_call(
         main_kernel,
@@ -416,10 +449,22 @@
             jax.ShapeDtypeStruct((2, TILES, 8, 128), f32),
             jax.ShapeDtypeStruct((2, NF, 4, 8, 128), f32),
         ),
-        in_specs=[vmem, vmem, smem, smem, vmem, hbm] + [vmem] * 9,
+        in_specs=[hbm] * 13 + [vmem] * 2,
         out_specs=(vmem, vmem, vmem),
         scratch_shapes=[
+            pltpu.VMEM((1, 64), jnp.int32),
+            pltpu.VMEM((1, 64), jnp.int32),
+            pltpu.SMEM((1,), jnp.int32),
+            pltpu.SMEM((2,), jnp.int32),
+            pltpu.VMEM((64, 1024), bf16),
             pltpu.VMEM((64, 128, 128), bf16),
+            pltpu.VMEM((32, 64), bf16),
+            pltpu.VMEM((64, 256), bf16),
+            pltpu.VMEM((64, 256), bf16),
+            pltpu.VMEM((1, 256), f32),
+            pltpu.VMEM((256, 256), bf16),
+            pltpu.VMEM((256, 256), bf16),
+            pltpu.VMEM((1, 256), f32),
             pltpu.VMEM((1, 64), jnp.int32),
             pltpu.SMEM((1, 64), jnp.int32),
             pltpu.VMEM((NF, 8, 128), f32),
@@ -434,12 +479,12 @@
             pltpu.VMEM((TILES, 8, 128), f32),
             pltpu.VMEM((NZ, 8, 128), f32),
             pltpu.VMEM((NZ, 8, 128), f32),
-            pltpu.SemaphoreType.DMA((2,)),
+            pltpu.SemaphoreType.DMA((14,)),
             pltpu.SemaphoreType.DMA((PHASES,)),
             pltpu.SemaphoreType.DMA((PHASES,)),
         ],
         compiler_params=pltpu.CompilerParams(
-            collective_id=1, has_side_effects=True, vmem_limit_bytes=32 * 2**20
+            collective_id=1, has_side_effects=True, vmem_limit_bytes=60 * 2**20
         ),
     )(
         block_target.reshape(1, 64),
@@ -448,14 +493,14 @@
         seed_rows,
         source_feats,
         block_values,
-        vertex_feats,
-        seed_weights,
+        vertex_feats.T,
         neigh_one,
         self_one,
         bias_one.reshape(1, 256),
         self_two,
         neigh_two,
         bias_two.reshape(1, 256),
+        seed_weights,
         output_grad,
     )
     outs = pl.pallas_call(
@@ -471,6 +516,7 @@
         ),
         in_specs=[vmem] * 3,
         out_specs=(vmem,) * 7,
+        compiler_params=pltpu.CompilerParams(vmem_limit_bytes=60 * 2**20),
     )(fin, gfin, out_two)
     out_two, neigh1, self1, bias1, self2, neigh2, bias2 = outs
     return out_two, neigh1, self1, bias1.reshape(256), self2, neigh2, bias2.reshape(256)

time: 76.6 us -> 63.5 us (0.83)
  local copies, waits for them, and re-layouts: 13.3 us -> 0 us
    unnamed x33 -> x0, local copies, waits for them, and re-layouts: 13.3 us -> none
where the time goes in v2:
time: 63.5 us; the launch traced here: 63.3 us
  Pallas kernels  62 us (98%)
  between operations  1.29 us (2%)
    pallas_call x1, Pallas kernels, body(): pl.pallas_call(main_kernel, out_shape=(jax.ShapeDtypeStruct((2, 256), bf1...  60.1 us
    pallas_call x1, Pallas kernels, body(): pl.pallas_call(lay_out_kernel, out_shape=(jax.ShapeDtypeStruct((2, 256),...  1.93 us

profile of v2, /device:TPU:1, one launch (start us, length us, event | category | flops | bytes accessed | tf_op | source)
XLA Modules:
  0.0 63.3 jit_solution(14555710542046657024)
XLA Ops:
  1.3 60.1 %shard_map.198 = (bf16[2,256]{1,0:T(2,128)(2,1)}, f32[2,21,8,128]{3,2,1,0:T(8,128)}, f32[2,16,4,8,128]{4,3,2,1,0:T(8,128)}) custom-call(s32[1,64]{1,0:T(1,128)} %bitcast.10, s32[1,64]{1,0:T(1,128)} %bitcast.11, s32[1]{0:T(128)S(6)} %copy.22.count_hbm, s32[2]{0:T(128)} %rows_hbm.1, bf16[64,1024]{1,0:T(8,128)(2,1)} %src_hbm.1, bf16[64,128,128]{2,1,0:T(8,128)(2,1)} %val_hbm.1, ...), custom_call_target="tpu_custom_call" | custom-call | tf_op jit(solution)/shard_map/pallas_call | solution.py:445
  61.4 1.9 %shard_map.199 = (bf16[2,256]{1,0:T(2,128)(2,1)}, f32[64,256]{1,0:T(8,128)}, f32[64,256]{1,0:T(8,128)}, f32[1,256]{1,0:T(1,128)}, f32[256,256]{1,0:T(8,128)}, /*index=5*/f32[256,256]{1,0:T(8,128)}, f32[1,256]{1,0:T(1,128)}) custom-call(f32[2,21,8,128]{3,2,1,0:T(8,128)} %get-tuple-element.17.fin_ref, f32[2,16,4,8,128]{4,3,2,1,0:T(8,128)} %get-tuple-element.18.gfin_ref, ...), custom_call_target="tpu_custom_call" | custom-call | tf_op jit(solution)/shard_map/pallas_call | solution.py:506

commit v3 on v2

v3 whole, which is shorter than its diff:
```python
import jax
import jax.numpy as jnp
from jax import lax
from jax.experimental import pallas as pl
from jax.experimental.pallas import tpu as pltpu
from jax.sharding import PartitionSpec as P

MESH = pl.DeviceIdType.MESH
HIGHEST = lax.Precision.HIGHEST
norm_eps = 1e-05
f32, bf16 = jnp.float32, jnp.bfloat16

NZ, NX, NF = 16, 4, 16
FAR_FIRST = (8, 7, 9, 6, 10, 5, 11, 4, 12, 3, 13, 2, 14, 1, 15)
FEAT_ORDER = (10, 2, 8, 6, 14, 9, 11, 5, 7, 13, 15, 1, 3, 4, 12)
BLOCK_ORDER = (4, 5, 3, 6, 2, 7, 1, 0)
(
    PAIR0, EARLY, OGZ, OGF, OGC, NBF, NBC, XY0, XY1, OWNC, VERTC, ZSUM0, AALL, ZSUM1, BALL, ZALL, FALL, FINC, GFINC,
) = (0,) + tuple(range(4, 22))
PHASES = 22


def dot(a, b, ca, cb, precision=None):
    return lax.dot_general(
        a, b, (((ca,), (cb,)), ((), ())), preferred_element_type=f32, precision=precision
    )


def main_kernel(
    target_hbm,
    source_hbm,
    count_hbm,
    rows_hbm,
    src_hbm,
    val_hbm,
    vert_hbm,
    neigh1_hbm,
    self1_hbm,
    bias1_hbm,
    self2_hbm,
    neigh2_hbm,
    bias2_hbm,
    sw_ref,
    og_ref,
    out_ref,
    bias_ref,
    fin_ref,
    gfin_ref,
    target_ref,
    source_ref,
    count_ref,
    rows_ref,
    src_ref,
    val,
    vert_ref,
    neigh1_ref,
    self1_ref,
    bias1_ref,
    self2_ref,
    neigh2_ref,
    bias2_ref,
    order_v,
    order_s,
    early,
    ogz,
    og_flat,
    nball,
    neigh_all,
    xy,
    ownt,
    vboth,
    agg,
    sib,
    zin,
    aall,
    rtile,
    zred,
    b_in,
    local_sem,
    ssem,
    rsem,
):
    g = lax.axis_index("graph")
    f = lax.axis_index("feat")
    z, c = g // 2, g % 2
    y, x = f // 4, f % 4
    sibling = (g + 1 - 2 * c, f)
    me = 16 * c + f

    def z_peer(off):
        return (2 * lax.rem(z + off, NZ) + c, f)

    def f_peer(off):
        return (g, lax.rem(f + off, NF))

    def f_across(off):
        return (g + 1 - 2 * c, lax.rem(f + off, NF))

    def x_peer(off):
        return (g, 4 * y + lax.rem(x + off, NX))

    def y_peer(off):
        return (g, 4 * lax.rem(y + off, NX) + x)

    def copy(src, dst, phase, dev):
        return pltpu.make_async_remote_copy(
            src_ref=src,
            dst_ref=dst,
            send_sem=ssem.at[phase],
            recv_sem=rsem.at[phase],
            device_id=dev,
            device_id_type=MESH,
        )

    pending = []

    def send(src, dst, phase, dev):
        copy(src, dst, phase, dev).start()

    def recv(ref, phase):
        pending.append((ref, phase))
        copy(ref, ref, phase, sibling).wait_recv()

    fetches = []
    for src, dst in (
        (target_hbm, target_ref),
        (source_hbm, source_ref),
        (count_hbm, count_ref),
        (val_hbm, val),
        (src_hbm, src_ref),
        (rows_hbm, rows_ref),
        (vert_hbm, vert_ref),
        (self1_hbm, self1_ref),
        (neigh1_hbm, neigh1_ref),
        (self2_hbm, self2_ref),
        (neigh2_hbm, neigh2_ref),
        (bias1_hbm, bias1_ref),
        (bias2_hbm, bias2_ref),
    ):
        fetches.append(pltpu.make_async_copy(src, dst, local_sem.at[1 + len(fetches)]))
        fetches[-1].start()

    barrier = pltpu.get_barrier_semaphore()

    def greet(dev):
        pl.semaphore_signal(barrier, inc=1, device_id=dev, device_id_type=MESH)

    for off in FAR_FIRST:
        greet(z_peer(off))
    for off in FEAT_ORDER:
        greet(f_peer(off))
        greet(f_across(off))
    greet(sibling)

    for i in range(3):
        fetches[i].wait()
    pair = target_ref[...] * 8 + source_ref[...]
    slot = lax.broadcasted_iota(jnp.int32, (64, 64), 1)
    code = jnp.where(slot >= count_ref[0], slot + 64, slot)
    hit = pair == lax.broadcasted_iota(jnp.int32, (64, 64), 0)
    picked = jnp.where(hit, code, 0)
    order_v[...] = jnp.sum(picked.T, axis=0, keepdims=True)
    to_scalar = pltpu.make_async_copy(order_v, order_s, local_sem.at[0])
    to_scalar.start()

    fetches[5].wait()
    hop = lax.broadcasted_iota(jnp.int32, (1, 32), 1)
    og_own = og_ref[...].astype(f32)
    sw_own = sw_ref[...].astype(f32)
    hot_own = jnp.concatenate(
        [(hop == rows_ref[0]).astype(f32), (hop == rows_ref[1]).astype(f32)], axis=0
    )
    gap = jnp.zeros((2, 32), f32)
    mix_own = jnp.where(
        c == 0,
        jnp.concatenate([sw_own, gap, hot_own, gap], axis=1),
        jnp.concatenate([gap, sw_own, gap, hot_own], axis=1),
    )
    og_rows = jnp.concatenate([og_own[:, 0:128], og_own[:, 128:256]], axis=0)
    early[me] = jnp.concatenate([og_rows, mix_own, jnp.zeros((2, 128), f32)], axis=0)
    ogz[me, z] = og_rows

    fetches[4].wait()
    doubled = jnp.concatenate([src_ref[...], src_ref[...]], axis=0)
    low_lanes = lax.broadcasted_iota(jnp.int32, (16, 128), 1) < 64
    to_scalar.wait()
    fetches[3].wait()

    for d in range(8):
        cols = []
        for s in range(8):
            k = order_s[0, d * 8 + s]
            live = jnp.where(k < 64, 1.0, 0.0).astype(bf16)
            cols.append(val[lax.rem(k, 64)] * live)
        wide = dot(jnp.concatenate(cols, axis=1), doubled, 1, 1)
        for q in range(4):
            top, bottom = wide[32 * q : 32 * q + 16], wide[32 * q + 16 : 32 * q + 32]
            agg[q % 2, 2 * d + q // 2] = jnp.where(low_lanes, top, bottom)

    for i in range(6, 13):
        fetches[i].wait()
    own_part = dot(vert_ref[...], self1_ref[...], 1, 0)
    xy[0, 0, x] = own_part[:, 0:128]
    xy[0, 1, y] = own_part[:, 128:256]
    vboth[c] = jnp.concatenate([vert_ref[...].astype(f32), jnp.zeros((32, 64), f32)], axis=1)
    nball[me] = neigh1_ref[pl.ds(pl.multiple_of(32 * c, 32), 32), :].astype(f32)

    pl.semaphore_wait(barrier, 46)

    block_rows = [2 * lax.rem(z // 2 + delta, 8) for delta in BLOCK_ORDER]
    for group in range(4):
        for row in block_rows[2 * group : 2 * group + 2]:
            send(agg.at[1 - c, pl.ds(row, 2)], sib.at[pl.ds(row, 2)], PAIR0 + group, sibling)
    for off in (2, 1, 3):
        send(xy.at[0, 0, x], xy.at[0, 0, x], XY0, x_peer(off))
        send(xy.at[0, 1, y], xy.at[0, 1, y], XY0, y_peer(off))
    for group in range(4):
        recv(sib.at[pl.ds(0, 4)], PAIR0 + group)
        for delta in BLOCK_ORDER[2 * group : 2 * group + 2]:
            row = 2 * lax.rem(z // 2 + delta, 8)
            if delta:
                for h in range(2):
                    agg[c, row + h] = agg[c, row + h] + sib[row + h]
                    send(agg.at[c, row + h], zin.at[z], ZSUM0, (2 * (row + h) + c, f))
            else:
                other = row + 1 - z % 2
                agg[c, other] = agg[c, other] + sib[other]
                send(agg.at[c, other], zin.at[z], ZSUM0, (2 * other + c, f))
                zin[z] = agg[c, z] + sib[z]
    for off in FEAT_ORDER:
        send(nball.at[me], nball.at[me], NBF, f_peer(off))
    for off in FEAT_ORDER:
        send(early.at[me], early.at[me], EARLY, f_peer(off))
        send(early.at[me], early.at[me], EARLY, f_across(off))
    send(early.at[me], early.at[me], EARLY, sibling)
    send(vboth.at[c], vboth.at[c], VERTC, sibling)

    recv(xy.at[0, :, pl.ds(0, 3)], XY0)
    xy[1, 0, y] = (xy[0, 0, 0] + xy[0, 0, 1]) + (xy[0, 0, 2] + xy[0, 0, 3])
    xy[1, 1, x] = (xy[0, 1, 0] + xy[0, 1, 1]) + (xy[0, 1, 2] + xy[0, 1, 3])
    for off in (2, 1, 3):
        send(xy.at[1, 0, y], xy.at[1, 0, y], XY1, y_peer(off))
        send(xy.at[1, 1, x], xy.at[1, 1, x], XY1, x_peer(off))
    for off in FAR_FIRST:
        send(ogz.at[me, z], ogz.at[me, z], OGZ, z_peer(off))

    recv(zin.at[pl.ds(0, NZ - 1)], ZSUM0)
    packed = [zin[i] for i in range(NZ)]
    while len(packed) > 1:
        packed = [packed[i] + packed[i + 1] for i in range(0, len(packed), 2)]
    aall[me] = packed[0]
    for off in FEAT_ORDER:
        send(aall.at[me], aall.at[me], AALL, f_peer(off))
        send(aall.at[me], aall.at[me], AALL, f_across(off))
    send(aall.at[me], aall.at[me], AALL, sibling)

    recv(nball.at[pl.ds(0, 15)], NBF)
    send(nball.at[pl.ds(16 * c, 16)], nball.at[pl.ds(16 * c, 16)], NBC, sibling)
    recv(xy.at[1, :, pl.ds(0, 3)], XY1)
    ownt[c, :, 0:128] = (xy[1, 0, 0] + xy[1, 0, 1]) + (xy[1, 0, 2] + xy[1, 0, 3])
    ownt[c, :, 128:256] = (xy[1, 1, 0] + xy[1, 1, 1]) + (xy[1, 1, 2] + xy[1, 1, 3])
    send(ownt.at[c], ownt.at[c], OWNC, sibling)

    recv(early.at[pl.ds(0, 31)], EARLY)
    groups = [(16 * core + 8 * half, r) for core in range(2) for half in range(2) for r in range(2)]
    og_64 = jnp.concatenate(
        [
            jnp.concatenate([early[i : i + 8, r, :], early[i : i + 8, 2 + r, :]], axis=1)
            for i, r in groups
        ],
        axis=0,
    ).astype(bf16)
    mix = jnp.concatenate([early[i : i + 8, 4 + r, :] for i, r in groups], axis=0)
    weight_mix, hot_mix = mix[:, 0:64], mix[:, 64:128]
    d_self = dot(og_64, self2_ref[...], 1, 1)
    d_agg = dot(og_64, neigh2_ref[...], 1, 1)
    d_hidden = dot(hot_mix, d_self, 0, 0, HIGHEST) + dot(weight_mix, d_agg, 0, 0, HIGHEST)
    mixer = jnp.where(f < 8, hot_mix, weight_mix).astype(bf16)

    recv(nball.at[pl.ds(0, 16)], NBC)
    for i in range(NF):
        for half in range(2):
            neigh_all[64 * i + 32 * half : 64 * i + 32 * half + 32, :] = nball[16 * half + i].astype(bf16)
    recv(ownt.at[0], OWNC)
    own_term = jnp.concatenate([ownt[0], ownt[1]], axis=0) + bias1_ref[...]
    recv(vboth.at[0], VERTC)
    vert_64 = jnp.concatenate([vboth[0], vboth[1]], axis=0)[:, 0:64]
    column = lax.broadcasted_iota(jnp.int32, (256, 128), 0)
    lane = lax.broadcasted_iota(jnp.int32, (256, 128), 1)
    chooser = (column == 32 * lax.rem(f, 8) + 16 * c + lane % 16).astype(f32).astype(bf16)

    recv(aall.at[pl.ds(0, 31)], AALL)
    sides = []
    for core in range(2):
        tops, bottoms = [], []
        for i in range(0, NF, 2):
            even, odd = aall[16 * core + i], aall[16 * core + i + 1]
            tops.append(jnp.where(low_lanes, even, pltpu.roll(odd, 64, 1)))
            bottoms.append(jnp.where(low_lanes, pltpu.roll(even, 64, 1), odd))
        sides += [jnp.concatenate(tops, axis=1), jnp.concatenate(bottoms, axis=1)]
    agg_64 = jnp.concatenate(sides, axis=0)
    agg_hi = agg_64.astype(bf16)
    agg_lo = (agg_64 - agg_hi.astype(f32)).astype(bf16)
    product = dot(jnp.concatenate([agg_hi, agg_lo], axis=0), neigh_all[...], 1, 0)
    pre_act = product[0:64] + product[64:128] + own_term

    rect = jnp.maximum(pre_act, 0.0)
    msq = jnp.mean(rect * rect, axis=-1, keepdims=True)
    inverse = lax.rsqrt(msq + norm_eps)
    hidden = (rect * inverse).astype(bf16)
    factor = jnp.mean(d_hidden * rect, axis=-1, keepdims=True) * inverse * inverse
    d_pre = jnp.where(pre_act > 0, (d_hidden - rect * factor) * inverse, 0.0)

    own0, own1 = aall[f], aall[16 + f]
    agg_own = jnp.concatenate([own0[:, 0:64], own0[:, 64:128], own1[:, 0:64], own1[:, 64:128]], axis=0)
    left_side = jnp.where(c == 0, agg_own, vert_64).astype(bf16)
    grad = dot(left_side, d_pre.astype(bf16), 0, 0)
    for a in range(8):
        for b in range(2):
            rtile[2 * a + b, 0:8] = grad[8 * a : 8 * a + 8, 128 * b : 128 * b + 128]

    chosen = dot(hidden, chooser, 1, 0).astype(bf16)
    mixed = dot(mixer, chosen, 1, 0)
    lane8 = lax.broadcasted_iota(jnp.int32, (8, 128), 1) // 16
    tile = jnp.zeros((8, 128), f32)
    for q in range(8):
        tile = jnp.where(lane8 == q, mixed[8 * q : 8 * q + 8], tile)
    tile = tile.astype(bf16).astype(f32)
    for i in range(NZ):
        rtile[i, 8:16] = tile
    for off in FAR_FIRST:
        to = lax.rem(z + off, NZ)
        send(rtile.at[to], zred.at[z], ZSUM1, (2 * to + c, f))
    zred[z] = rtile[z]
    recv(ogz.at[me, pl.ds(0, NZ - 1)], OGZ)
    for off in FEAT_ORDER:
        send(ogz.at[me], ogz.at[me], OGF, f_peer(off))
    bias1_part = jnp.sum(d_pre, axis=0, keepdims=True)
    b_in[z] = jnp.concatenate([bias1_part[:, 0:128], bias1_part[:, 128:256]], axis=0)
    for off in FAR_FIRST:
        send(b_in.at[z], b_in.at[z], BALL, z_peer(off))

    mix_8 = jnp.concatenate([mix_own, jnp.zeros((6, 128), f32)], axis=0).astype(bf16)
    self_vals = dot(mix_8[:, 64:128], hidden, 1, 0).astype(bf16)
    agg_two = dot(mix_8[:, 0:64], hidden, 1, 0).astype(bf16)
    out_full = dot(self_vals, self2_ref[...], 1, 0) + dot(agg_two, neigh2_ref[...], 1, 0)
    out_ref[...] = (out_full + bias2_ref[...]).astype(bf16)[0:2]

    recv(ogz.at[pl.ds(0, NF - 1)], OGF)
    send(ogz.at[pl.ds(16 * c, 16)], ogz.at[pl.ds(16 * c, 16)], OGC, sibling)
    recv(zred.at[pl.ds(0, NZ - 1)], ZSUM1)
    parts = [zred[i, 0:8] for i in range(NZ)]
    while len(parts) > 1:
        parts = [parts[i] + parts[i + 1] for i in range(0, len(parts), 2)]
    fin_ref[c, z] = parts[0]
    for off in FAR_FIRST:
        send(fin_ref.at[c, z], fin_ref.at[c, z], ZALL, z_peer(off))

    recv(ogz.at[pl.ds(0, NF)], OGC)
    total2 = jnp.zeros((16, 256), f32)
    for q, (first, r) in enumerate(groups):
        for i in range(8):
            piece = jnp.concatenate([ogz[first + i, :, r, :], ogz[first + i, :, 2 + r, :]], axis=1)
            total2 = total2 + piece
            og_flat[128 * q + 16 * i : 128 * q + 16 * i + 16, :] = piece.astype(bf16)
    bias2_sum = jnp.sum(total2, axis=0, keepdims=True)

    columns = jnp.concatenate([zred[:, 8 + i, :] for i in range(8)], axis=0).T.astype(bf16)
    columns = jnp.concatenate([columns[16 * q : 16 * q + 16] for q in range(8)], axis=1)
    share = dot(columns, og_flat[...], 1, 0)
    for a in range(2):
        for b in range(2):
            gfin_ref[me, 2 * a + b] = share[8 * a : 8 * a + 8, 128 * b : 128 * b + 128]
    for off in FEAT_ORDER:
        send(gfin_ref.at[me], gfin_ref.at[me], FALL, f_peer(off))
    recv(b_in.at[pl.ds(0, NZ - 1)], BALL)
    bias1_sum = b_in[0]
    for i in range(1, NZ):
        bias1_sum = bias1_sum + b_in[i]
    bias_ref[...] = jnp.concatenate(
        [bias1_sum, bias2_sum[:, 0:128], bias2_sum[:, 128:256], jnp.zeros((4, 128), f32)], axis=0
    )

    recv(gfin_ref.at[pl.ds(0, NF - 1)], FALL)
    send(gfin_ref.at[pl.ds(16 * c, 16)], gfin_ref.at[pl.ds(16 * c, 16)], GFINC, sibling)
    recv(fin_ref.at[c, pl.ds(0, NZ - 1)], ZALL)
    send(fin_ref.at[c], fin_ref.at[c], FINC, sibling)
    recv(gfin_ref.at[pl.ds(0, NF)], GFINC)
    recv(fin_ref.at[1 - c], FINC)

    for ref, phase in pending:
        copy(ref, ref, phase, sibling).wait_send()


def lay_out_kernel(
    fin_ref, gfin_ref, out_in_ref, bias_ref, out_ref, neigh1_ref, self1_ref, bias1_ref, self2_ref, neigh2_ref, bias2_ref
):
    out_ref[...] = out_in_ref[...]
    for a in range(8):
        for b in range(2):
            rows, cols = slice(8 * a, 8 * a + 8), slice(128 * b, 128 * b + 128)
            neigh1_ref[rows, cols] = fin_ref[0, 2 * a + b]
            self1_ref[rows, cols] = fin_ref[1, 2 * a + b]
    bias = bias_ref[...]
    bias1_ref[...] = jnp.concatenate([bias[0:1], bias[1:2]], axis=1)
    bias2_ref[...] = jnp.concatenate([bias[2:3], bias[3:4]], axis=1)
    for i in range(NF):
        ref = self2_ref if i < 8 else neigh2_ref
        for core in range(2):
            for t in range(4):
                row = 32 * (i % 8) + 16 * core + 8 * (t // 2)
                col = 128 * (t % 2)
                ref[row : row + 8, col : col + 128] = gfin_ref[16 * core + i, t]


def body(
    source_feats,
    vertex_feats,
    block_values,
    block_target,
    block_source,
    block_count,
    seed_rows,
    seed_weights,
    neigh_one,
    self_one,
    bias_one,
    self_two,
    neigh_two,
    bias_two,
    output_grad,
):
    vmem = pl.BlockSpec(memory_space=pltpu.VMEM)
    hbm = pl.BlockSpec(memory_space=pl.ANY)
    out_two, bias, fin, gfin = pl.pallas_call(
        main_kernel,
        out_shape=(
            jax.ShapeDtypeStruct((2, 256), bf16),
            jax.ShapeDtypeStruct((8, 128), f32),
            jax.ShapeDtypeStruct((2, NZ, 8, 128), f32),
            jax.ShapeDtypeStruct((2 * NF, 4, 8, 128), f32),
        ),
        in_specs=[hbm] * 13 + [vmem] * 2,
        out_specs=(vmem,) * 4,
        scratch_shapes=[
            pltpu.VMEM((1, 64), jnp.int32),
            pltpu.VMEM((1, 64), jnp.int32),
            pltpu.SMEM((1,), jnp.int32),
            pltpu.SMEM((2,), jnp.int32),
            pltpu.VMEM((64, 1024), bf16),
            pltpu.VMEM((64, 128, 128), bf16),
            pltpu.VMEM((32, 64), bf16),
            pltpu.VMEM((64, 256), bf16),
            pltpu.VMEM((64, 256), bf16),
            pltpu.VMEM((1, 256), f32),
            pltpu.VMEM((256, 256), bf16),
            pltpu.VMEM((256, 256), bf16),
            pltpu.VMEM((1, 256), f32),
            pltpu.VMEM((1, 64), jnp.int32),
            pltpu.SMEM((1, 64), jnp.int32),
            pltpu.VMEM((2 * NF, 8, 128), f32),
            pltpu.VMEM((2 * NF, NZ, 4, 128), f32),
            pltpu.VMEM((1024, 256), bf16),
            pltpu.VMEM((2 * NF, 32, 256), f32),
            pltpu.VMEM((1024, 256), bf16),
            pltpu.VMEM((2, 2, NX, 32, 128), f32),
            pltpu.VMEM((2, 32, 256), f32),
            pltpu.VMEM((2, 32, 128), f32),
            pltpu.VMEM((2, NZ, 16, 128), f32),
            pltpu.VMEM((NZ, 16, 128), f32),
            pltpu.VMEM((NZ, 16, 128), f32),
            pltpu.VMEM((2 * NF, 16, 128), f32),
            pltpu.VMEM((NZ, 16, 128), f32),
            pltpu.VMEM((NZ, 16, 128), f32),
            pltpu.VMEM((NZ, 2, 128), f32),
            pltpu.SemaphoreType.DMA((14,)),
            pltpu.SemaphoreType.DMA((PHASES,)),
            pltpu.SemaphoreType.DMA((PHASES,)),
        ],
        compiler_params=pltpu.CompilerParams(
            collective_id=1, has_side_effects=True, vmem_limit_bytes=60 * 2**20
        ),
    )(
        block_target.reshape(1, 64),
        block_source.reshape(1, 64),
        block_count,
        seed_rows,
        source_feats,
        block_values,
        vertex_feats.T,
        neigh_one,
        self_one,
        bias_one.reshape(1, 256),
        self_two,
        neigh_two,
        bias_two.reshape(1, 256),
        seed_weights,
        output_grad,
    )
    outs = pl.pallas_call(
        lay_out_kernel,
        out_shape=(
            jax.ShapeDtypeStruct((2, 256), bf16),
            jax.ShapeDtypeStruct((64, 256), f32),
            jax.ShapeDtypeStruct((64, 256), f32),
            jax.ShapeDtypeStruct((1, 256), f32),
            jax.ShapeDtypeStruct((256, 256), f32),
            jax.ShapeDtypeStruct((256, 256), f32),
            jax.ShapeDtypeStruct((1, 256), f32),
        ),
        in_specs=[vmem] * 4,
        out_specs=(vmem,) * 7,
        compiler_params=pltpu.CompilerParams(vmem_limit_bytes=60 * 2**20),
    )(fin, gfin, out_two, bias)
    out_two, neigh1, self1, bias1, self2, neigh2, bias2 = outs
    return out_two, neigh1, self1, bias1.reshape(256), self2, neigh2, bias2.reshape(256)


def solution(mesh):
    in_specs = (
        P("feat", "graph"),
        P("feat", "graph"),
        P("graph", None, None),
        P("graph"),
        P("graph"),
        P("graph"),
        P(("graph", "feat")),
        P(("graph", "feat"), None),
        P("feat", None),
        P("feat", None),
        P(),
        P(),
        P(),
        P(),
        P(("graph", "feat"), None),
    )
    out_specs = (P(("graph", "feat"), None), P("feat", None), P("feat", None), P(), P(), P(), P())
    return jax.shard_map(body, mesh=mesh, in_specs=in_specs, out_specs=out_specs, check_vma=False)
```

time: 63.5 us -> 57.8 us (0.910)
  Pallas kernels: 62 us -> 56.3 us
    pallas_call x1, Pallas kernels: 60.1 us -> 54.4 us  [body(): pl.pallas_call(main_kernel, out_shape=(jax.ShapeDtypeStruct((2, 256), bf1...]
where the time goes in v3:
time: 57.8 us; the launch traced here: 57.6 us
  Pallas kernels  56.3 us (97%)
  between operations  1.29 us (2%)
    pallas_call x1, Pallas kernels, body(): pl.pallas_call(main_kernel, out_shape=(jax.ShapeDtypeStruct((2, 256), bf1...  54.4 us
    pallas_call x1, Pallas kernels, body(): pl.pallas_call(lay_out_kernel, out_shape=(jax.ShapeDtypeStruct((2, 256),...  1.92 us

profile of v3, /device:TPU:1, one launch (start us, length us, event | category | flops | bytes accessed | tf_op | source)
XLA Modules:
  0.0 57.6 jit_solution(4198047058549492082)
XLA Ops:
  1.3 54.4 %shard_map.198 = (bf16[2,256]{1,0:T(2,128)(2,1)}, f32[8,128]{1,0:T(8,128)}, f32[2,16,8,128]{3,2,1,0:T(8,128)}, f32[32,4,8,128]{3,2,1,0:T(8,128)}) custom-call(s32[1,64]{1,0:T(1,128)} %bitcast.10, s32[1,64]{1,0:T(1,128)} %bitcast.11, s32[1]{0:T(128)S(6)} %copy.22.count_hbm, s32[2]{0:T(128)} %rows_hbm.1, bf16[64,1024]{1,0:T(8,128)(2,1)} %src_hbm.1, ...), custom_call_target="tpu_custom_call" | custom-call | tf_op jit(solution)/shard_map/pallas_call | solution.py:435
  55.7 1.9 %shard_map.199 = (bf16[2,256]{1,0:T(2,128)(2,1)}, f32[64,256]{1,0:T(8,128)}, f32[64,256]{1,0:T(8,128)}, f32[1,256]{1,0:T(1,128)}, f32[256,256]{1,0:T(8,128)}, /*index=5*/f32[256,256]{1,0:T(8,128)}, f32[1,256]{1,0:T(1,128)}) custom-call(f32[2,16,8,128]{3,2,1,0:T(8,128)} %get-tuple-element.18.fin_ref, f32[32,4,8,128]{3,2,1,0:T(8,128)} %get-tuple-element.19.gfin_ref, ...), custom_call_target="tpu_custom_call" | custom-call | tf_op jit(solution)/shard_map/pallas_call | solution.py:500

commit v4 on v3

--- a/solution.py
+++ b/solution.py
@@ -15,9 +15,9 @@
 FEAT_ORDER = (10, 2, 8, 6, 14, 9, 11, 5, 7, 13, 15, 1, 3, 4, 12)
 BLOCK_ORDER = (4, 5, 3, 6, 2, 7, 1, 0)
 (
-    PAIR0, EARLY, OGZ, OGF, OGC, NBF, NBC, XY0, XY1, OWNC, VERTC, ZSUM0, AALL, ZSUM1, BALL, ZALL, FALL, FINC, GFINC,
+    PAIR0, EARLY, OGZ, OGF, OGC, NBF, NBC, XY0, XY1, OWNC, VERTC, ZSUM0, AALL, ZSUM1, BALL, ZALL, FINC, GFINC, FALL,
 ) = (0,) + tuple(range(4, 22))
-PHASES = 22
+PHASES = 25
 
 
 def dot(a, b, ca, cb, precision=None):
@@ -42,10 +42,15 @@
     bias2_hbm,
     sw_ref,
     og_ref,
+    out_hbm,
+    bias1_out,
+    bias2_out,
+    fin_hbm,
+    g2_hbm,
     out_ref,
     bias_ref,
     fin_ref,
-    gfin_ref,
+    g2_ref,
     target_ref,
     source_ref,
     count_ref,
@@ -77,6 +82,7 @@
     zred,
     b_in,
     local_sem,
+    put_sem,
     ssem,
     rsem,
 ):
@@ -139,6 +145,12 @@
     ):
         fetches.append(pltpu.make_async_copy(src, dst, local_sem.at[1 + len(fetches)]))
         fetches[-1].start()
+
+    puts = []
+
+    def put(src, dst):
+        puts.append(pltpu.make_async_copy(src, dst, put_sem.at[len(puts)]))
+        puts[-1].start()
 
     barrier = pltpu.get_barrier_semaphore()
 
@@ -289,6 +301,10 @@
     lane = lax.broadcasted_iota(jnp.int32, (256, 128), 1)
     chooser = (column == 32 * lax.rem(f, 8) + 16 * c + lane % 16).astype(f32).astype(bf16)
 
+    recv(ogz.at[me, pl.ds(0, NZ - 1)], OGZ)
+    for off in FEAT_ORDER:
+        send(ogz.at[me], ogz.at[me], OGF, f_peer(off))
+
     recv(aall.at[pl.ds(0, 31)], AALL)
     sides = []
     for core in range(2):
@@ -332,29 +348,20 @@
         to = lax.rem(z + off, NZ)
         send(rtile.at[to], zred.at[z], ZSUM1, (2 * to + c, f))
     zred[z] = rtile[z]
-    recv(ogz.at[me, pl.ds(0, NZ - 1)], OGZ)
-    for off in FEAT_ORDER:
-        send(ogz.at[me], ogz.at[me], OGF, f_peer(off))
     bias1_part = jnp.sum(d_pre, axis=0, keepdims=True)
     b_in[z] = jnp.concatenate([bias1_part[:, 0:128], bias1_part[:, 128:256]], axis=0)
     for off in FAR_FIRST:
         send(b_in.at[z], b_in.at[z], BALL, z_peer(off))
 
+    recv(ogz.at[pl.ds(0, NF - 1)], OGF)
+    send(ogz.at[pl.ds(16 * c, 16)], ogz.at[pl.ds(16 * c, 16)], OGC, sibling)
+
     mix_8 = jnp.concatenate([mix_own, jnp.zeros((6, 128), f32)], axis=0).astype(bf16)
     self_vals = dot(mix_8[:, 64:128], hidden, 1, 0).astype(bf16)
     agg_two = dot(mix_8[:, 0:64], hidden, 1, 0).astype(bf16)
     out_full = dot(self_vals, self2_ref[...], 1, 0) + dot(agg_two, neigh2_ref[...], 1, 0)
-    out_ref[...] = (out_full + bias2_ref[...]).astype(bf16)[0:2]
-
-    recv(ogz.at[pl.ds(0, NF - 1)], OGF)
-    send(ogz.at[pl.ds(16 * c, 16)], ogz.at[pl.ds(16 * c, 16)], OGC, sibling)
-    recv(zred.at[pl.ds(0, NZ - 1)], ZSUM1)
-    parts = [zred[i, 0:8] for i in range(NZ)]
-    while len(parts) > 1:
-        parts = [parts[i] + parts[i + 1] for i in range(0, len(parts), 2)]
-    fin_ref[c, z] = parts[0]
-    for off in FAR_FIRST:
-        send(fin_ref.at[c, z], fin_ref.at[c, z], ZALL, z_peer(off))
+    out_ref[...] = (out_full + bias2_ref[...]).astype(bf16).astype(f32)[0:2]
+    put(out_ref, out_hbm)
 
     recv(ogz.at[pl.ds(0, NF)], OGC)
     total2 = jnp.zeros((16, 256), f32)
@@ -365,52 +372,66 @@
             og_flat[128 * q + 16 * i : 128 * q + 16 * i + 16, :] = piece.astype(bf16)
     bias2_sum = jnp.sum(total2, axis=0, keepdims=True)
 
+    recv(zred.at[pl.ds(0, NZ - 1)], ZSUM1)
+    parts = [zred[i, 0:8] for i in range(NZ)]
+    while len(parts) > 1:
+        parts = [parts[i] + parts[i + 1] for i in range(0, len(parts), 2)]
+    own_tile = fin_ref.at[
+        c, pl.ds(pl.multiple_of(8 * (z // 2), 8), 8), pl.ds(pl.multiple_of(128 * lax.rem(z, 2), 128), 128)
+    ]
+    own_tile[...] = parts[0]
+    for off in FAR_FIRST:
+        send(own_tile, own_tile, ZALL, z_peer(off))
+
     columns = jnp.concatenate([zred[:, 8 + i, :] for i in range(8)], axis=0).T.astype(bf16)
     columns = jnp.concatenate([columns[16 * q : 16 * q + 16] for q in range(8)], axis=1)
     share = dot(columns, og_flat[...], 1, 0)
-    for a in range(2):
-        for b in range(2):
-            gfin_ref[me, 2 * a + b] = share[8 * a : 8 * a + 8, 128 * b : 128 * b + 128]
-    for off in FEAT_ORDER:
-        send(gfin_ref.at[me], gfin_ref.at[me], FALL, f_peer(off))
+    own_rows = g2_ref.at[f // 8, lax.rem(f, 8), c]
+    own_rows[...] = share
+    for dy in (2, 1, 3, 0):
+        for dx in (2, 1, 3, 0):
+            if dy or dx:
+                to = (g, 4 * lax.rem(y + dy, NX) + lax.rem(x + dx, NX))
+                send(own_rows, own_rows, FALL + dy, to)
     recv(b_in.at[pl.ds(0, NZ - 1)], BALL)
     bias1_sum = b_in[0]
     for i in range(1, NZ):
         bias1_sum = bias1_sum + b_in[i]
-    bias_ref[...] = jnp.concatenate(
-        [bias1_sum, bias2_sum[:, 0:128], bias2_sum[:, 128:256], jnp.zeros((4, 128), f32)], axis=0
-    )
-
-    recv(gfin_ref.at[pl.ds(0, NF - 1)], FALL)
-    send(gfin_ref.at[pl.ds(16 * c, 16)], gfin_ref.at[pl.ds(16 * c, 16)], GFINC, sibling)
-    recv(fin_ref.at[c, pl.ds(0, NZ - 1)], ZALL)
+    bias_ref[0] = jnp.concatenate([bias1_sum[0:1], bias1_sum[1:2]], axis=1)
+    bias_ref[1] = bias2_sum
+    put(bias_ref.at[0], bias1_out)
+    put(bias_ref.at[1], bias2_out)
+
+    for dy in (0, 1, 3, 2):
+        recv(g2_ref.at[0, pl.ds(0, 4 if dy else 3), 0], FALL + dy)
+        row = lax.rem(y + NX - dy, NX)
+        here = (row // 2, pl.ds(4 * lax.rem(row, 2), 4), c)
+        send(g2_ref.at[here], g2_ref.at[here], GFINC, sibling)
+        put(g2_ref.at[here], g2_hbm.at[here])
+    recv(zred.at[pl.ds(0, NZ - 1), pl.ds(0, 8)], ZALL)
     send(fin_ref.at[c], fin_ref.at[c], FINC, sibling)
-    recv(gfin_ref.at[pl.ds(0, NF)], GFINC)
+    put(fin_ref.at[c], fin_hbm.at[c])
+    recv(g2_ref.at[:, :, 0], GFINC)
+    put(g2_ref.at[:, :, 1 - c], g2_hbm.at[:, :, 1 - c])
     recv(fin_ref.at[1 - c], FINC)
+    put(fin_ref.at[1 - c], fin_hbm.at[1 - c])
+    for one in puts:
+        one.wait()
 
     for ref, phase in pending:
         copy(ref, ref, phase, sibling).wait_send()
 
 
 def lay_out_kernel(
-    fin_ref, gfin_ref, out_in_ref, bias_ref, out_ref, neigh1_ref, self1_ref, bias1_ref, self2_ref, neigh2_ref, bias2_ref
+    out_in_ref, b1_in, b2_in, fin_in, g2_in, out_ref, neigh1_ref, self1_ref, bias1_ref, self2_ref, neigh2_ref, bias2_ref
 ):
-    out_ref[...] = out_in_ref[...]
-    for a in range(8):
-        for b in range(2):
-            rows, cols = slice(8 * a, 8 * a + 8), slice(128 * b, 128 * b + 128)
-            neigh1_ref[rows, cols] = fin_ref[0, 2 * a + b]
-            self1_ref[rows, cols] = fin_ref[1, 2 * a + b]
-    bias = bias_ref[...]
-    bias1_ref[...] = jnp.concatenate([bias[0:1], bias[1:2]], axis=1)
-    bias2_ref[...] = jnp.concatenate([bias[2:3], bias[3:4]], axis=1)
-    for i in range(NF):
-        ref = self2_ref if i < 8 else neigh2_ref
-        for core in range(2):
-            for t in range(4):
-                row = 32 * (i % 8) + 16 * core + 8 * (t // 2)
-                col = 128 * (t % 2)
-                ref[row : row + 8, col : col + 128] = gfin_ref[16 * core + i, t]
+    out_ref[...] = out_in_ref[...].astype(bf16)
+    neigh1_ref[...] = fin_in[0]
+    self1_ref[...] = fin_in[1]
+    bias1_ref[...] = b1_in[...]
+    bias2_ref[...] = b2_in[...]
+    self2_ref[...] = g2_in[0]
+    neigh2_ref[...] = g2_in[1]
 
 
 def body(
@@ -432,17 +453,22 @@
 ):
     vmem = pl.BlockSpec(memory_space=pltpu.VMEM)
     hbm = pl.BlockSpec(memory_space=pl.ANY)
-    out_two, bias, fin, gfin = pl.pallas_call(
+    out_two, bias1, bias2, fin, g2 = pl.pallas_call(
         main_kernel,
         out_shape=(
-            jax.ShapeDtypeStruct((2, 256), bf16),
-            jax.ShapeDtypeStruct((8, 128), f32),
-            jax.ShapeDtypeStruct((2, NZ, 8, 128), f32),
-            jax.ShapeDtypeStruct((2 * NF, 4, 8, 128), f32),
+            jax.ShapeDtypeStruct((2, 256), f32),
+            jax.ShapeDtypeStruct((1, 256), f32),
+            jax.ShapeDtypeStruct((1, 256), f32),
+            jax.ShapeDtypeStruct((2, 64, 256), f32),
+            jax.ShapeDtypeStruct((2, 8, 2, 16, 256), f32),
         ),
         in_specs=[hbm] * 13 + [vmem] * 2,
-        out_specs=(vmem,) * 4,
+        out_specs=(hbm,) * 5,
         scratch_shapes=[
+            pltpu.VMEM((2, 256), f32),
+            pltpu.VMEM((2, 1, 256), f32),
+            pltpu.VMEM((2, 64, 256), f32),
+            pltpu.VMEM((2, 8, 2, 16, 256), f32),
             pltpu.VMEM((1, 64), jnp.int32),
             pltpu.VMEM((1, 64), jnp.int32),
             pltpu.SMEM((1,), jnp.int32),
@@ -474,6 +500,7 @@
             pltpu.VMEM((NZ, 16, 128), f32),
             pltpu.VMEM((NZ, 2, 128), f32),
             pltpu.SemaphoreType.DMA((14,)),
+            pltpu.SemaphoreType.DMA((10,)),
             pltpu.SemaphoreType.DMA((PHASES,)),
             pltpu.SemaphoreType.DMA((PHASES,)),
         ],
@@ -508,10 +535,10 @@
             jax.ShapeDtypeStruct((256, 256), f32),
             jax.ShapeDtypeStruct((1, 256), f32),
         ),
-        in_specs=[vmem] * 4,
+        in_specs=[vmem] * 5,
         out_specs=(vmem,) * 7,
         compiler_params=pltpu.CompilerParams(vmem_limit_bytes=60 * 2**20),
-    )(fin, gfin, out_two, bias)
+    )(out_two, bias1, bias2, fin, g2.reshape(2, 256, 256))
     out_two, neigh1, self1, bias1, self2, neigh2, bias2 = outs
     return out_two, neigh1, self1, bias1.reshape(256), self2, neigh2, bias2.reshape(256)
 

time: 57.8 us -> 57.1 us (0.988)
  Pallas kernels: 56.3 us -> 55.6 us
    pallas_call x1, Pallas kernels: 54.4 us -> 53.6 us  [body(): pl.pallas_call(main_kernel, out_shape=(jax.ShapeDtypeStruct((2, 256), f32...]
where the time goes in v4:
time: 57.1 us; the launch traced here: 56.9 us
  Pallas kernels  55.6 us (97%)
  between operations  1.29 us (2%)
    pallas_call x1, Pallas kernels, body(): pl.pallas_call(main_kernel, out_shape=(jax.ShapeDtypeStruct((2, 256), f32...  53.6 us
    pallas_call x1, Pallas kernels, body(): pl.pallas_call(lay_out_kernel, out_shape=(jax.ShapeDtypeStruct((2, 256),...  1.98 us

profile of v4, /device:TPU:1, one launch (start us, length us, event | category | flops | bytes accessed | tf_op | source)
XLA Modules:
  0.0 56.9 jit_solution(14634651352920424633)
XLA Ops:
  1.3 53.6 %shard_map.198 = (f32[2,256]{1,0:T(2,128)}, f32[1,256]{1,0:T(1,128)}, f32[1,256]{1,0:T(1,128)}, f32[2,64,256]{2,1,0:T(8,128)}, f32[2,8,2,16,256]{4,3,2,1,0:T(8,128)}) custom-call(s32[1,64]{1,0:T(1,128)} %bitcast.12, s32[1,64]{1,0:T(1,128)} %bitcast.13, s32[1]{0:T(128)S(6)} %copy.22.count_hbm, s32[2]{0:T(128)} %rows_hbm.1, bf16[64,1024]{1,0:T(8,128)(2,1)} %src_hbm.1, ...), custom_call_target="tpu_custom_call" | custom-call | tf_op jit(solution)/shard_map/pallas_call | solution.py:456
  54.9 2.0 %shard_map.199 = (bf16[2,256]{1,0:T(2,128)(2,1)}, f32[64,256]{1,0:T(8,128)}, f32[64,256]{1,0:T(8,128)}, f32[1,256]{1,0:T(1,128)}, f32[256,256]{1,0:T(8,128)}, /*index=5*/f32[256,256]{1,0:T(8,128)}, f32[1,256]{1,0:T(1,128)}) custom-call(f32[2,256]{1,0:T(2,128)} %get-tuple-element.19.out_in_ref, f32[1,256]{1,0:T(1,128)} %get-tuple-element.20.b1_in, ...), custom_call_target="tpu_custom_call" | custom-call | tf_op jit(solution)/shard_map/pallas_call | solution.py:527

commit v5 on v4

--- a/solution.py
+++ b/solution.py
@@ -15,9 +15,10 @@
 FEAT_ORDER = (10, 2, 8, 6, 14, 9, 11, 5, 7, 13, 15, 1, 3, 4, 12)
 BLOCK_ORDER = (4, 5, 3, 6, 2, 7, 1, 0)
 (
-    PAIR0, EARLY, OGZ, OGF, OGC, NBF, NBC, XY0, XY1, OWNC, VERTC, ZSUM0, AALL, ZSUM1, BALL, ZALL, FINC, GFINC, FALL,
-) = (0,) + tuple(range(4, 22))
-PHASES = 25
+    PAIR0, EARLY, EARLYC, OGZ, OGF, OGC, NBF, NBC, XY0, XY1, OWNC, VERTC, ZSUM0, AALL, AALLC, ZSUM1, BALL, ZALL,
+    FINC, GFINC, FALL,
+) = (0,) + tuple(range(4, 24))
+PHASES = 27
 
 
 def dot(a, b, ca, cb, precision=None):
@@ -99,9 +100,6 @@
     def f_peer(off):
         return (g, lax.rem(f + off, NF))
 
-    def f_across(off):
-        return (g + 1 - 2 * c, lax.rem(f + off, NF))
-
     def x_peer(off):
         return (g, 4 * y + lax.rem(x + off, NX))
 
@@ -161,7 +159,6 @@
         greet(z_peer(off))
     for off in FEAT_ORDER:
         greet(f_peer(off))
-        greet(f_across(off))
     greet(sibling)
 
     for i in range(3):
@@ -217,7 +214,7 @@
     vboth[c] = jnp.concatenate([vert_ref[...].astype(f32), jnp.zeros((32, 64), f32)], axis=1)
     nball[me] = neigh1_ref[pl.ds(pl.multiple_of(32 * c, 32), 32), :].astype(f32)
 
-    pl.semaphore_wait(barrier, 46)
+    pl.semaphore_wait(barrier, 31)
 
     block_rows = [2 * lax.rem(z // 2 + delta, 8) for delta in BLOCK_ORDER]
     for group in range(4):
@@ -243,8 +240,6 @@
         send(nball.at[me], nball.at[me], NBF, f_peer(off))
     for off in FEAT_ORDER:
         send(early.at[me], early.at[me], EARLY, f_peer(off))
-        send(early.at[me], early.at[me], EARLY, f_across(off))
-    send(early.at[me], early.at[me], EARLY, sibling)
     send(vboth.at[c], vboth.at[c], VERTC, sibling)
 
     recv(xy.at[0, :, pl.ds(0, 3)], XY0)
@@ -263,8 +258,6 @@
     aall[me] = packed[0]
     for off in FEAT_ORDER:
         send(aall.at[me], aall.at[me], AALL, f_peer(off))
-        send(aall.at[me], aall.at[me], AALL, f_across(off))
-    send(aall.at[me], aall.at[me], AALL, sibling)
 
     recv(nball.at[pl.ds(0, 15)], NBF)
     send(nball.at[pl.ds(16 * c, 16)], nball.at[pl.ds(16 * c, 16)], NBC, sibling)
@@ -273,7 +266,9 @@
     ownt[c, :, 128:256] = (xy[1, 1, 0] + xy[1, 1, 1]) + (xy[1, 1, 2] + xy[1, 1, 3])
     send(ownt.at[c], ownt.at[c], OWNC, sibling)
 
-    recv(early.at[pl.ds(0, 31)], EARLY)
+    recv(early.at[pl.ds(0, 15)], EARLY)
+    send(early.at[pl.ds(16 * c, 16)], early.at[pl.ds(16 * c, 16)], EARLYC, sibling)
+    recv(early.at[pl.ds(0, 16)], EARLYC)
     groups = [(16 * core + 8 * half, r) for core in range(2) for half in range(2) for r in range(2)]
     og_64 = jnp.concatenate(
         [
@@ -305,7 +300,9 @@
     for off in FEAT_ORDER:
         send(ogz.at[me], ogz.at[me], OGF, f_peer(off))
 
-    recv(aall.at[pl.ds(0, 31)], AALL)
+    recv(aall.at[pl.ds(0, 15)], AALL)
+    send(aall.at[pl.ds(16 * c, 16)], aall.at[pl.ds(16 * c, 16)], AALLC, sibling)
+    recv(aall.at[pl.ds(0, 16)], AALLC)
     sides = []
     for core in range(2):
         tops, bottoms = [], []

time: 57.1 us -> 56.2 us (0.984)
  Pallas kernels: 55.6 us -> 54.7 us
    pallas_call x1, Pallas kernels: 53.6 us -> 52.8 us  [body(): pl.pallas_call(main_kernel, out_shape=(jax.ShapeDtypeStruct((2, 256), f32...]
where the time goes in v5:
time: 56.2 us; the launch traced here: 56 us
  Pallas kernels  54.7 us (97%)
  between operations  1.29 us (2%)
    pallas_call x1, Pallas kernels, body(): pl.pallas_call(main_kernel, out_shape=(jax.ShapeDtypeStruct((2, 256), f32...  52.8 us
    pallas_call x1, Pallas kernels, body(): pl.pallas_call(lay_out_kernel, out_shape=(jax.ShapeDtypeStruct((2, 256),...  1.98 us

profile of v5, /device:TPU:1, one launch (start us, length us, event | category | flops | bytes accessed | tf_op | source)
XLA Modules:
  0.0 56.0 jit_solution(10108271549921897364)
XLA Ops:
  1.3 52.8 %shard_map.198 = (f32[2,256]{1,0:T(2,128)}, f32[1,256]{1,0:T(1,128)}, f32[1,256]{1,0:T(1,128)}, f32[2,64,256]{2,1,0:T(8,128)}, f32[2,8,2,16,256]{4,3,2,1,0:T(8,128)}) custom-call(s32[1,64]{1,0:T(1,128)} %bitcast.12, s32[1,64]{1,0:T(1,128)} %bitcast.13, s32[1]{0:T(128)S(6)} %copy.22.count_hbm, s32[2]{0:T(128)} %rows_hbm.1, bf16[64,1024]{1,0:T(8,128)(2,1)} %src_hbm.1, ...), custom_call_target="tpu_custom_call" | custom-call | tf_op jit(solution)/shard_map/pallas_call | solution.py:453
  54.1 2.0 %shard_map.199 = (bf16[2,256]{1,0:T(2,128)(2,1)}, f32[64,256]{1,0:T(8,128)}, f32[64,256]{1,0:T(8,128)}, f32[1,256]{1,0:T(1,128)}, f32[256,256]{1,0:T(8,128)}, /*index=5*/f32[256,256]{1,0:T(8,128)}, f32[1,256]{1,0:T(1,128)}) custom-call(f32[2,256]{1,0:T(2,128)} %get-tuple-element.19.out_in_ref, f32[1,256]{1,0:T(1,128)} %get-tuple-element.20.b1_in, ...), custom_call_target="tpu_custom_call" | custom-call | tf_op jit(solution)/shard_map/pallas_call | solution.py:524

commit v6 on v5

--- a/solution.py
+++ b/solution.py
@@ -195,7 +195,8 @@
     to_scalar.wait()
     fetches[3].wait()
 
-    for d in range(8):
+    for p, delta in enumerate(BLOCK_ORDER):
+        d = lax.rem(z // 2 + delta, 8)
         cols = []
         for s in range(8):
             k = order_s[0, d * 8 + s]
@@ -204,7 +205,7 @@
         wide = dot(jnp.concatenate(cols, axis=1), doubled, 1, 1)
         for q in range(4):
             top, bottom = wide[32 * q : 32 * q + 16], wide[32 * q + 16 : 32 * q + 32]
-            agg[q % 2, 2 * d + q // 2] = jnp.where(low_lanes, top, bottom)
+            agg[q % 2, 2 * p + q // 2] = jnp.where(low_lanes, top, bottom)
 
     for i in range(6, 13):
         fetches[i].wait()
@@ -216,26 +217,25 @@
 
     pl.semaphore_wait(barrier, 31)
 
-    block_rows = [2 * lax.rem(z // 2 + delta, 8) for delta in BLOCK_ORDER]
     for group in range(4):
-        for row in block_rows[2 * group : 2 * group + 2]:
-            send(agg.at[1 - c, pl.ds(row, 2)], sib.at[pl.ds(row, 2)], PAIR0 + group, sibling)
+        piece = pl.ds(4 * group, 4)
+        send(agg.at[1 - c, piece], sib.at[piece], PAIR0 + group, sibling)
     for off in (2, 1, 3):
         send(xy.at[0, 0, x], xy.at[0, 0, x], XY0, x_peer(off))
         send(xy.at[0, 1, y], xy.at[0, 1, y], XY0, y_peer(off))
     for group in range(4):
         recv(sib.at[pl.ds(0, 4)], PAIR0 + group)
-        for delta in BLOCK_ORDER[2 * group : 2 * group + 2]:
-            row = 2 * lax.rem(z // 2 + delta, 8)
-            if delta:
+        for p in (2 * group, 2 * group + 1):
+            chip = 2 * lax.rem(z // 2 + BLOCK_ORDER[p], 8)
+            if BLOCK_ORDER[p]:
                 for h in range(2):
-                    agg[c, row + h] = agg[c, row + h] + sib[row + h]
-                    send(agg.at[c, row + h], zin.at[z], ZSUM0, (2 * (row + h) + c, f))
+                    agg[c, 2 * p + h] = agg[c, 2 * p + h] + sib[2 * p + h]
+                    send(agg.at[c, 2 * p + h], zin.at[z], ZSUM0, (2 * (chip + h) + c, f))
             else:
-                other = row + 1 - z % 2
-                agg[c, other] = agg[c, other] + sib[other]
-                send(agg.at[c, other], zin.at[z], ZSUM0, (2 * other + c, f))
-                zin[z] = agg[c, z] + sib[z]
+                h, mine = 1 - z % 2, z % 2
+                agg[c, 2 * p + h] = agg[c, 2 * p + h] + sib[2 * p + h]
+                send(agg.at[c, 2 * p + h], zin.at[z], ZSUM0, (2 * (chip + h) + c, f))
+                zin[z] = agg[c, 2 * p + mine] + sib[2 * p + mine]
     for off in FEAT_ORDER:
         send(nball.at[me], nball.at[me], NBF, f_peer(off))
     for off in FEAT_ORDER:

time: 56.2 us -> 56.5 us (level)
  no operation moved by 1% of the time
where the time goes in v6:
time: 56.5 us; the launch traced here: 56.3 us
  Pallas kernels  55 us (97%)
  between operations  1.29 us (2%)
    pallas_call x1, Pallas kernels, body(): pl.pallas_call(main_kernel, out_shape=(jax.ShapeDtypeStruct((2, 256), f32...  53 us
    pallas_call x1, Pallas kernels, body(): pl.pallas_call(lay_out_kernel, out_shape=(jax.ShapeDtypeStruct((2, 256),...  1.98 us

profile of v6, /device:TPU:1, one launch (start us, length us, event | category | flops | bytes accessed | tf_op | source)
XLA Modules:
  0.0 56.3 jit_solution(17091474144176463064)
XLA Ops:
  1.3 53.0 %shard_map.198 = (f32[2,256]{1,0:T(2,128)}, f32[1,256]{1,0:T(1,128)}, f32[1,256]{1,0:T(1,128)}, f32[2,64,256]{2,1,0:T(8,128)}, f32[2,8,2,16,256]{4,3,2,1,0:T(8,128)}) custom-call(s32[1,64]{1,0:T(1,128)} %bitcast.12, s32[1,64]{1,0:T(1,128)} %bitcast.13, s32[1]{0:T(128)S(6)} %copy.22.count_hbm, s32[2]{0:T(128)} %rows_hbm.1, bf16[64,1024]{1,0:T(8,128)(2,1)} %src_hbm.1, ...), custom_call_target="tpu_custom_call" | custom-call | tf_op jit(solution)/shard_map/pallas_call | solution.py:453
  54.3 2.0 %shard_map.199 = (bf16[2,256]{1,0:T(2,128)(2,1)}, f32[64,256]{1,0:T(8,128)}, f32[64,256]{1,0:T(8,128)}, f32[1,256]{1,0:T(1,128)}, f32[256,256]{1,0:T(8,128)}, /*index=5*/f32[256,256]{1,0:T(8,128)}, f32[1,256]{1,0:T(1,128)}) custom-call(f32[2,256]{1,0:T(2,128)} %get-tuple-element.19.out_in_ref, f32[1,256]{1,0:T(1,128)} %get-tuple-element.20.b1_in, ...), custom_call_target="tpu_custom_call" | custom-call | tf_op jit(solution)/shard_map/pallas_call | solution.py:524
